TPU v7x, 32 devices: a whole 2x2x4 slice. The times are simulated.
32 devices in a mesh: groups: 2 (over y), seq: 4 (over z), head: 2 (over x), batch: 2 (over core).
Axes of the slice: x: 2, y: 2, z: 4, core: 2. Of those that a mesh axis runs over, the one named last changes fastest.
Arguments:
- query_rows: bfloat16 [4, 4096, 1024], P(('groups', 'batch'), 'seq', 'head'), parts along dimension 0, may hold values from -32 to 32
- key_rows: bfloat16 [4, 4096, 1024], P(('groups', 'batch'), 'seq', 'head'), parts along dimension 0, may hold values from -32 to 32
- value_rows: bfloat16 [4, 4096, 1024], P(('groups', 'batch'), 'seq', 'head'), parts along dimension 0, may hold values from -6 to 6
- grad_output: bfloat16 [4, 4096, 1024], P(('groups', 'batch'), 'seq', 'head'), parts along dimension 0, may hold values from -6 to 6
Outputs:
- grad_queries: bfloat16 [4, 4096, 1024], P(('groups', 'batch'), 'seq', 'head'), parts along dimension 0
- grad_keys: bfloat16 [4, 4096, 1024], P(('groups', 'batch'), 'seq', 'head'), parts along dimension 0
- grad_values: bfloat16 [4, 4096, 1024], P(('groups', 'batch'), 'seq', 'head'), parts along dimension 0
There are 2 independent parts, one for each index of `groups`. A program takes and returns all parts, laid end to end along the dimension named above; each array names one. Nothing has to cross between parts.
All inputs are finite; a program needn't handle non-finite values. Where the computation divides by a largest or mean magnitude, that divisor is 1e-20 or more.
Results may differ from a plain program's by a relative error of at most 0.023.
The roundings to bfloat16 on the way count: a program that leaves them out, or rounds other values in their place, can miss the bound.
Values may be sent and summed in bfloat16 or wider, within the bound.
A program may use at most 128 MiB of HBM per device.

v0:
```python
import jax
import jax.numpy as jnp
from jax import lax
from jax.sharding import PartitionSpec as P

DH = 64
M = 256
ITERS = 4


def joined(x, axis, combine):
    everything = jax.tree.map(lambda part: lax.all_gather(part, axis), x)
    leading = jax.tree.map(lambda part: part[0], everything)

    def turn(k, so_far):
        return combine(so_far, jax.tree.map(lambda part: part[k], everything))

    return lax.fori_loop(1, lax.axis_size(axis), turn, leading)


def newton(matrix):
    size = matrix.shape[-1]
    identity = jnp.eye(size, dtype=matrix.dtype)
    col_norm = jnp.max(jnp.sum(jnp.abs(matrix), axis=-2), axis=-1)
    row_norm = jnp.max(jnp.sum(jnp.abs(matrix), axis=-1), axis=-1)
    approx = jnp.swapaxes(matrix, -1, -2) / (col_norm * row_norm)[..., None, None]
    for sweep in range(ITERS):
        product = jnp.matmul(matrix, approx, precision=lax.Precision.HIGHEST)
        inner = jnp.matmul(product, 7.0 * identity - product, precision=lax.Precision.HIGHEST)
        inner = jnp.matmul(product, 15.0 * identity - inner, precision=lax.Precision.HIGHEST)
        approx = 0.25 * jnp.matmul(approx, 13.0 * identity - inner, precision=lax.Precision.HIGHEST)
    return approx


def normalize(scores):
    shifted = jnp.exp(scores - jnp.max(scores, axis=-1, keepdims=True))
    return shifted / jnp.sum(shifted, axis=-1, keepdims=True)


def combine_stats(first, second):
    top = jnp.maximum(first[0], second[0])
    total = first[1] * jnp.exp(first[0] - top) + second[1] * jnp.exp(second[0] - top)
    return (top, total)


def per_device(query_rows, key_rows, value_rows, grad_output):
    high = lax.Precision.HIGHEST
    count, rows, width = query_rows.shape
    heads = width // DH
    spread = lax.axis_size("seq")
    land_dev = M // spread
    seg_len = rows // land_dev
    temper = DH ** (-0.5)

    def landmarks(data):
        summed = jnp.sum(data.reshape(count, land_dev, seg_len, width), axis=2, dtype=jnp.float32)
        return (summed / seg_len).astype(jnp.bfloat16)

    land_q, land_k = (
        lax.all_gather(landmarks(query_rows), "seq", axis=1, tiled=True),
        lax.all_gather(landmarks(key_rows), "seq", axis=1, tiled=True),
    )
    quer = query_rows.reshape(count, rows, heads, DH)
    keys_four = key_rows.reshape(count, rows, heads, DH)
    vals_four = value_rows.reshape(count, rows, heads, DH)
    grad_four = grad_output.reshape(count, rows, heads, DH)
    landq_four = land_q.reshape(count, M, heads, DH)
    landk_four = land_k.reshape(count, M, heads, DH)
    soft_f = normalize(
        temper * jnp.einsum("blhd,bmhd->bhlm", quer, landk_four, preferred_element_type=jnp.float32)
    )
    soft_a = normalize(
        temper
        * jnp.einsum("bmhd,bnhd->bhmn", landq_four, landk_four, preferred_element_type=jnp.float32)
    )
    inverse, pull = jax.vjp(newton, soft_a)
    scores_b = temper * jnp.einsum(
        "bmhd,blhd->bhml", landq_four, keys_four, preferred_element_type=jnp.float32
    )
    local_max = jnp.max(scores_b, axis=-1)
    local_sum = jnp.sum(jnp.exp(scores_b - local_max[..., None]), axis=-1)
    top, total = joined((local_max, local_sum), "seq", combine_stats)
    soft_b = jnp.exp(scores_b - top[..., None]) / total[..., None]
    weights_b = soft_b.astype(jnp.bfloat16)
    mix_part = jnp.einsum(
        "bhml,blhd->bmhd", weights_b, vals_four, preferred_element_type=jnp.float32
    ).reshape(count, M, width)
    weights_f = soft_f.astype(jnp.bfloat16)
    comb_part = jnp.einsum(
        "bhlm,blhd->bmhd", weights_f, grad_four, preferred_element_type=jnp.float32
    ).reshape(count, M, width)
    mixed = lax.psum(mix_part, "seq")
    grad_comb = lax.psum(comb_part, "seq")
    mixed_four = mixed.reshape(count, M, heads, DH)
    gcomb_four = grad_comb.reshape(count, M, heads, DH)
    combined = jnp.einsum("bhmn,bnhd->bmhd", inverse, mixed_four, precision=high).astype(
        jnp.bfloat16
    )
    grad_f = jnp.einsum("blhd,bmhd->bhlm", grad_four, combined, preferred_element_type=jnp.float32)
    dsf = (soft_f * (grad_f - jnp.sum(grad_f * soft_f, axis=-1, keepdims=True))).astype(
        jnp.bfloat16
    )
    dq_local = temper * jnp.einsum(
        "bhlm,bmhd->blhd", dsf, landk_four, preferred_element_type=jnp.float32
    )
    key_part = temper * jnp.einsum("bhlm,blhd->bmhd", dsf, quer, preferred_element_type=jnp.float32)
    grad_inv = jnp.einsum("bmhd,bnhd->bhmn", gcomb_four, mixed_four, precision=high)
    grad_mix = jnp.einsum("bhnm,bnhd->bmhd", inverse, gcomb_four, precision=high)
    grad_a = pull(grad_inv)[0]
    dsa = soft_a * (grad_a - jnp.sum(grad_a * soft_a, axis=-1, keepdims=True))
    query_land_a = temper * jnp.einsum(
        "bhmn,bnhd->bmhd", dsa, landk_four.astype(jnp.float32), precision=high
    )
    key_land_a = temper * jnp.einsum(
        "bhmn,bmhd->bnhd", dsa, landq_four.astype(jnp.float32), precision=high
    )
    gmix = grad_mix.astype(jnp.bfloat16)
    grad_b = jnp.einsum("bmhd,blhd->bhml", gmix, vals_four, preferred_element_type=jnp.float32)
    row_dot = jnp.einsum("bmhd,bmhd->bhm", gmix.astype(jnp.float32), mixed_four)
    dsb = (soft_b * (grad_b - row_dot[..., None])).astype(jnp.bfloat16)
    grad_vals = jnp.einsum("bhml,bmhd->blhd", weights_b, gmix, preferred_element_type=jnp.float32)
    query_part = temper * jnp.einsum(
        "bhml,blhd->bmhd", dsb, keys_four, preferred_element_type=jnp.float32
    )
    dk_local = temper * jnp.einsum(
        "bhml,bmhd->blhd", dsb, landq_four, preferred_element_type=jnp.float32
    )
    query_part = query_part.reshape(count, M, width)
    key_part = key_part.reshape(count, M, width)
    start = lax.axis_index("seq") * land_dev
    total_q, total_k = lax.psum((query_part, key_part), "seq")
    own_q = lax.dynamic_slice_in_dim(total_q, start, land_dev, 1)
    own_k = lax.dynamic_slice_in_dim(total_k, start, land_dev, 1)
    own_qa = lax.dynamic_slice_in_dim(query_land_a.reshape(count, M, width), start, land_dev, 1)
    own_ka = lax.dynamic_slice_in_dim(key_land_a.reshape(count, M, width), start, land_dev, 1)
    query_land = (own_q + own_qa) / seg_len
    key_land = (own_k + own_ka) / seg_len
    grad_q = dq_local.reshape(count, land_dev, seg_len, width) + query_land[:, :, None, :]
    grad_k = dk_local.reshape(count, land_dev, seg_len, width) + key_land[:, :, None, :]
    grad_queries = grad_q.reshape(count, rows, width).astype(jnp.bfloat16)
    grad_keys = grad_k.reshape(count, rows, width).astype(jnp.bfloat16)
    grad_values = grad_vals.reshape(count, rows, width).astype(jnp.bfloat16)
    return (grad_queries, grad_keys, grad_values)


def solution(mesh):
    return jax.shard_map(
        per_device,
        mesh=mesh,
        in_specs=(
            P(("groups", "batch"), "seq", "head"),
            P(("groups", "batch"), "seq", "head"),
            P(("groups", "batch"), "seq", "head"),
            P(("groups", "batch"), "seq", "head"),
        ),
        out_specs=(
            P(("groups", "batch"), "seq", "head"),
            P(("groups", "batch"), "seq", "head"),
            P(("groups", "batch"), "seq", "head"),
        ),
        check_vma=False,
    )
```

profile of v0, /device:TPU:0, one launch (start us, length us, event | category | flops | bytes accessed | tf_op | source)
XLA Modules:
  0.0 380.3 jit_solution(17328483483391836617)
XLA Ops:
  10.2 15.6 %all-gather.1 = bf16[256,512]{1,0:T(8,128)(2,1)S(1)} all-gather(bf16[64,512]{1,0:T(8,128)(2,1)S(1)} %multiply_convert_fusion.1), channel_id=3, replica_groups=mesh['groups'=2,'seq'=4,'head'=2,'batch'=2] {'seq'}, dimensions={0}, use_global_device_ids=true | all-gather | bytes 327680 | tf_op jit(solution)/shard_map/all_gather | solution.py:60
  26.0 14.6 %all-gather = bf16[256,512]{1,0:T(8,128)(2,1)S(1)} all-gather(bf16[64,512]{1,0:T(8,128)(2,1)S(1)} %multiply_convert_fusion.2), channel_id=2, replica_groups=mesh['groups'=2,'seq'=4,'head'=2,'batch'=2] {'seq'}, dimensions={0}, use_global_device_ids=true | all-gather | bytes 327680 | tf_op jit(solution)/shard_map/all_gather | solution.py:61
  40.7 2.4 copy.89
  43.1 2.3 copy.93
  46.7 13.1 %all-gather.2 = f32[32,256]{1,0:T(8,128)S(1)} all-gather(f32[8,256]{1,0:T(8,128)S(1)} %get-tuple-element.173), channel_id=4, replica_groups=mesh['groups'=2,'seq'=4,'head'=2,'batch'=2] {'seq'}, dimensions={0}, use_global_device_ids=true | all-gather | bytes 40960 | tf_op jit(solution)/shard_map/all_gather | solution.py:12
  61.7 13.1 %all-gather.3 = f32[32,256]{1,0:T(8,128)S(1)} all-gather(f32[8,256]{1,0:T(8,128)S(1)} %exponential_reduce_fusion), channel_id=5, replica_groups=mesh['groups'=2,'seq'=4,'head'=2,'batch'=2] {'seq'}, dimensions={0}, use_global_device_ids=true | all-gather | bytes 40960 | tf_op jit(solution)/shard_map/all_gather | solution.py:12
  74.9 5.0 %fusion.216 = (f32[8,1024]{1,0:T(8,128)S(1)}, f32[8,1024,256]{1,2,0:T(8,128)}) fusion(bf16[256,8,64]{0,2,1:T(8,128)(2,1)S(1)} %bitcast.289, bf16[1024,8,64]{0,2,1:T(8,128)(2,1)S(1)} %bitcast.287), kind=kOutput, calls=%fused_computation.218 | convolution fusion | flops 274727168 | bytes 9732096 | tf_op jit(solution)/shard_map/sub | solution.py:36
  79.9 6.2 %fusion.139 = f32[256,8,64]{0,2,1:T(8,128)} fusion(bf16[1024,8,64]{0,2,1:T(8,128)(2,1)S(1)} %bitcast.297, f32[8,256,1024]{2,1,0:T(8,128)} %copy-done.18, f32[8,256]{1,0:T(8,128)S(1)} %bitcast.303, f32[8,256]{1,0:T(8,128)S(1)} %bitcast.300), kind=kOutput, calls=%fused_computation.149 | convolution fusion | flops 276824064 | bytes 9977856 | tf_op jit(solution)/shard_map/bhml,blhd->bmhd/dot_general | solution.py:85
  93.0 2.9 copy.91
  95.9 8.1 %online-softmax = f32[8,256,256]{2,1,0:T(8,128)} custom-call(f32[8,256,256]{2,1,0:T(8,128)} %copy-done, f32[8,256,256]{2,1,0:T(8,128)} %copy.91), custom_call_target="tpu_custom_call" | custom-call | tf_op online-softmax
  104.0 4.6 %fusion.28 = f32[8,256,256]{2,1,0:T(8,128)S(1)} fusion(f32[8,256,256]{2,1,0:T(8,128)} %online-softmax, f32[256,256]{1,0:T(8,128)S(1)} %fusion.193), kind=kOutput, calls=%fused_computation.38 | convolution fusion | flops 1611137024 | bytes 4456448 | tf_op jit(solution)/shard_map/jvp()/dot_general | solution.py:29
  108.6 2.3 fusion.108
  112.2 5.4 %fusion.116 = f32[8,256,256]{2,1,0:T(8,128)} fusion(f32[8,256,256]{2,1,0:T(8,128)S(1)} %fusion.108, f32[256,256]{1,0:T(8,128)S(1)} %fusion.195, f32[8]{0:T(128)S(1)} %get-tuple-element.168, f32[8,256,256]{2,1,0:T(8,128)S(1)} %copy-done.1, f32[8,256]{1,0:T(8,128)S(1)} %fusion.115, f32[8,256]{1,0:T(8,128)S(1)} %get-tuple-element.177), kind=kOutput, calls=%fused_computation.141 | convolution fusion | flops 1613234176 | bytes 6570016 | tf_op jit(solution)/shard_map/jvp()/dot_general | solution.py:31
  117.7 8.4 %online-softmax.1 = f32[8,256,256]{2,1,0:T(8,128)} custom-call(f32[8,256,256]{2,1,0:T(8,128)} %copy-done, f32[8,256,256]{2,1,0:T(8,128)} %fusion.116), custom_call_target="tpu_custom_call" | custom-call | tf_op online-softmax
  126.1 4.6 %fusion.24 = f32[8,256,256]{2,1,0:T(8,128)S(1)} fusion(f32[8,256,256]{2,1,0:T(8,128)} %online-softmax.1, f32[256,256]{1,0:T(8,128)S(1)} %fusion.193), kind=kOutput, calls=%fused_computation.34 | convolution fusion | flops 1611137024 | bytes 4456448 | tf_op jit(solution)/shard_map/jvp()/dot_general | solution.py:29
  130.7 2.3 fusion.101
  134.3 3.6 fusion.122
  137.9 8.5 %online-softmax.2 = f32[8,256,256]{2,1,0:T(8,128)} custom-call(f32[8,256,256]{2,1,0:T(8,128)} %copy-done, f32[8,256,256]{2,1,0:T(8,128)} %fusion.122), custom_call_target="tpu_custom_call" | custom-call | tf_op online-softmax
  146.4 4.6 %fusion.20 = f32[8,256,256]{2,1,0:T(8,128)S(1)} fusion(f32[8,256,256]{2,1,0:T(8,128)} %online-softmax.2, f32[256,256]{1,0:T(8,128)S(1)} %fusion.193), kind=kOutput, calls=%fused_computation.30 | convolution fusion | flops 1611137024 | bytes 4456448 | tf_op jit(solution)/shard_map/jvp()/dot_general | solution.py:29
  151.0 2.3 fusion.94
  154.7 3.6 fusion.125
  158.3 8.2 %online-softmax.3 = f32[8,256,256]{2,1,0:T(8,128)} custom-call(f32[8,256,256]{2,1,0:T(8,128)} %copy-done, f32[8,256,256]{2,1,0:T(8,128)} %fusion.125), custom_call_target="tpu_custom_call" | custom-call | tf_op online-softmax
  166.5 5.9 %fusion.16 = f32[8,256,256]{2,1,0:T(8,128)} fusion(f32[8,256,256]{2,1,0:T(8,128)} %online-softmax.3, f32[256,256]{1,0:T(8,128)S(1)} %fusion.193), kind=kOutput, calls=%fused_computation.26 | convolution fusion | flops 1611137024 | bytes 4456448 | tf_op jit(solution)/shard_map/jvp()/dot_general | solution.py:29
  172.6 4.0 %fusion.87 = f32[8,256,256]{2,1,0:T(8,128)S(1)} fusion(f32[8,256,256]{2,1,0:T(8,128)S(1)} %copy-done.9, f32[8,256,256]{2,1,0:T(8,128)} %fusion.16, f32[256,256]{1,0:T(8,128)S(1)} %fusion.194), kind=kOutput, calls=%fused_computation.114 | convolution fusion | flops 1611137024 | bytes 6553600 | tf_op jit(solution)/shard_map/jvp()/dot_general | solution.py:30
  177.9 3.5 fusion.84
  181.4 3.9 %fusion.157 = bf16[256,8,64]{0,2,1:T(8,128)(2,1)S(1)} fusion(f32[256,8,64]{0,2,1:T(8,128)} %get-tuple-element.161, f32[8,256,256]{2,1,0:T(8,128)} %fusion.84), kind=kOutput, calls=%fused_computation.157 | convolution fusion | flops 403308544 | bytes 2883584 | tf_op jit(solution)/shard_map/bhmn,bnhd->bmhd/dot_general | solution.py:96
  185.4 2.6 fusion.190
  189.9 5.9 %fusion.136 = bf16[8,64,1024]{2,1,0:T(8,128)(2,1)} fusion(bf16[8,64,256]{2,1,0:T(8,128)(2,1)S(1)} %get-tuple-element.186, f32[8,256,1024]{2,1,0:T(8,128)} %copy-done.18, f32[8,256]{1,0:T(8,128)S(1)} %bitcast.304, f32[8,256]{1,0:T(8,128)S(1)} %bitcast.301), kind=kOutput, calls=%fused_computation.148 | convolution fusion | flops 277348352 | bytes 9715712 | tf_op jit(solution)/shard_map/bhml,bmhd->blhd/dot_general | solution.py:121
  195.9 3.4 multiply_convert_fusion
  201.5 2.2 convolution_multiply_fusion
  203.7 3.5 fusion.77
  207.3 2.2 fusion.73
  209.5 3.5 fusion.71
  213.0 2.7 fusion.14
  215.7 3.5 negate_add_fusion.3
  219.2 3.4 fusion.219
  222.7 4.4 %fusion.208 = f32[8,256,256]{2,1,0:T(8,128)S(1)} fusion(f32[8,256,256]{2,1,0:T(8,128)S(1)} %negate_add_fusion.3, f32[8,256,256]{2,1,0:T(8,128)S(1)} %copy-done.2, f32[8,256]{1,0:T(8,128)S(1)} %fusion.115, f32[8,256]{1,0:T(8,128)S(1)} %get-tuple-element.177), kind=kOutput, calls=%fused_computation.216 | convolution fusion | flops 1611661312 | bytes 6307840 | tf_op jit(solution)/shard_map/transpose(jvp())/dot_general | solution.py:28
  227.1 2.4 add_multiply_fusion.2
  231.7 3.5 fusion.220
  235.2 2.2 fusion.66
  237.5 3.9 %fusion.64 = f32[8,256,256]{2,1,0:T(8,128)S(1)} fusion(f32[8,256,256]{2,1,0:T(8,128)S(1)} %copy-done.8, f32[8,256,256]{2,1,0:T(8,128)S(1)} %fusion.220), kind=kOutput, calls=%fused_computation.91 | convolution fusion | flops 1611137024 | bytes 6291456 | tf_op jit(solution)/shard_map/transpose(jvp())/dot_general | solution.py:30
  243.6 3.5 negate_add_fusion.2
  247.1 3.5 fusion.221
  250.6 4.4 %add_multiply_fusion.1 = f32[8,256,256]{2,1,0:T(8,128)S(1)} fusion(f32[8,256,256]{2,1,0:T(8,128)S(1)} %fusion.89, f32[8,256,256]{2,1,0:T(8,128)S(1)} %negate_add_fusion.2, f32[8,256,256]{2,1,0:T(8,128)S(1)} %copy-done.2, f32[8,256]{1,0:T(8,128)S(1)} %fusion.115, f32[8,256]{1,0:T(8,128)S(1)} %get-tuple-element.177), kind=kOutput, calls=%fused_computation.65 | convolution fusion | flops 1612709888 | bytes 8404992 | tf_op jit(solution)/shard_map/transpose(jvp())/dot_general | solution.py:28
  257.2 3.5 fusion.222
  260.7 2.3 fusion.59
  263.0 3.5 fusion.57
  266.5 2.4 fusion.22
  269.0 3.5 negate_add_fusion.1
  272.5 3.4 fusion.223
  275.9 4.3 %add_multiply_fusion = f32[8,256,256]{2,1,0:T(8,128)S(1)} fusion(f32[8,256,256]{2,1,0:T(8,128)S(1)} %fusion.96, f32[8,256,256]{2,1,0:T(8,128)S(1)} %negate_add_fusion.1, f32[8,256,256]{2,1,0:T(8,128)S(1)} %copy-done.2, f32[8,256]{1,0:T(8,128)S(1)} %fusion.115, f32[8,256]{1,0:T(8,128)S(1)} %get-tuple-element.177), kind=kOutput, calls=%fused_computation.63 | convolution fusion | flops 1612709888 | bytes 8404992 | tf_op jit(solution)/shard_map/transpose(jvp())/dot_general | solution.py:28
  280.2 3.2 fusion.202
  285.7 3.5 fusion.50
  291.4 3.5 negate_add_fusion
  295.0 5.5 %fusion.212 = f32[8,256,256]{1,2,0:T(8,128)} fusion(f32[8,256,256]{2,1,0:T(8,128)S(1)} %negate_add_fusion, f32[8,256,256]{2,1,0:T(8,128)S(1)} %copy-done.2, f32[8,256]{1,0:T(8,128)S(1)} %fusion.115, f32[8,256]{1,0:T(8,128)S(1)} %get-tuple-element.177), kind=kOutput, calls=%fused_computation.217 | convolution fusion | flops 1611661312 | bytes 6307840 | tf_op jit(solution)/shard_map/transpose(jvp())/dot_general | solution.py:28
  302.1 2.6 fusion.5
  308.6 4.0 %fusion.41 = (f32[8]{0:T(128)S(1)}, f32[8,256,256]{1,2,0:T(8,128)}) fusion(f32[8]{0:T(128)S(1)} %get-tuple-element.167, f32[8,256]{1,0:T(8,128)S(1)} %fusion.115, f32[8,256,256]{2,1,0:T(8,128)S(1)} %copy-done.2, f32[8,256]{1,0:T(8,128)S(1)} %get-tuple-element.177, f32[8,256,256]{1,2,0:T(8,128)S(1)} %copy-done.53, f32[8,256,256]{2,1,0:T(8,128)S(1)} %add_multiply_fusion, ...), kind=kOutput, calls=%fused_computation.58 | convolution fusion | flops 1614282752 | bytes 10764352 | tf_op jit(solution)/shard_map/transpose(jvp())/dot_general | solution.py:31
  312.8 7.9 %fusion.42 = (f32[8,256]{1,0:T(8,128)S(1)}, f32[1,8,256,256]{3,2,1,0:T(8,128)}) fusion(f32[8,256]{1,0:T(8,128)S(1)} %fusion.115, f32[8,256,256]{2,1,0:T(8,128)S(1)} %copy-done.2, f32[8,256]{1,0:T(8,128)S(1)} %get-tuple-element.177, f32[8,256]{1,0:T(8,128)S(1)} %broadcast_select_fusion, f32[8,256]{1,0:T(8,128)S(1)} %broadcast_select_fusion.1, ...), kind=kOutput, calls=%fused_computation.61 | convolution fusion | flops 1622669312 | bytes 14721056 | tf_op jit(solution)/shard_map/transpose(jvp())/dot_general | solution.py:28
  322.9 2.9 copy.122
  325.8 2.3 copy.123
  328.1 2.9 copy.119
  331.0 4.0 %fusion.148 = f32[8,64,256]{2,1,0:T(8,128)} fusion(bf16[256,8,64]{0,2,1:T(8,128)(2,1)S(1)} %bitcast.284, f32[1,8,256,256]{3,2,1,0:T(8,128)} %get-tuple-element.184, f32[8,256]{1,0:T(8,128)S(1)} %get-tuple-element.183, f32[8,256,256]{2,1,0:T(8,128)S(1)} %copy-done.2, f32[8,256]{1,0:T(8,128)S(1)} %fusion.115, f32[8,256]{1,0:T(8,128)S(1)} %get-tuple-element.177), kind=kOutput, calls=%fused_computation.152 | convolution fusion | flops 404881408 | bytes 5005312 | tf_op jit(solution)/shard_map/bhmn,bmhd->bnhd/dot_general | solution.py:114
  335.0 2.4 fusion.145
  337.3 28.7 %all-reduce.5.cloned.1.call-done = (f32[1,256,512]{1,2,0:T(8,128)}, f32[1,256,512]{1,2,0:T(8,128)}) async-done(((f32[1,256,512]{1,2,0:T(8,128)}, f32[1,256,512]{1,2,0:T(8,128)}), (f32[1,256,512]{1,2,0:T(8,128)}, f32[1,256,512]{1,2,0:T(8,128)})) %all-reduce.5.cloned.1.call-update) | async-done | bytes 1048592 | tf_op jit(solution)/shard_map/psum | solution.py:131
  (174 shorter events, 49.1 us)
Async XLA Ops:
  7.2 1.7 copy-start.39
  7.2 2.1 copy-start.40
  7.2 174.3 %all-reduce.7.cloned.1.call-start = ((), (), s32[]{:S(2)}) async-start(), calls=%async_computation.1 | async-start | bytes 2097152 | tf_op jit(solution)/shard_map/psum | solution.py:92
  8.9 36.5 %copy-start.33 = (bf16[1,1024,512]{1,2,0:T(8,128)(2,1)}, bf16[1,1024,512]{1,2,0:T(8,128)(2,1)S(1)}, u32[]{:S(2)}) copy-start(bf16[1,1024,512]{1,2,0:T(8,128)(2,1)S(1)} %copy.88) | copy-start | bytes 3145732
  9.8 65.1 %copy-start.41 = (bf16[1,1024,512]{1,2,0:T(8,128)(2,1)}, bf16[1,1024,512]{1,2,0:T(8,128)(2,1)S(1)}, u32[]{:S(2)}) copy-start(bf16[1,1024,512]{1,2,0:T(8,128)(2,1)S(1)} %copy.86) | copy-start | bytes 3145732
  40.7 48.0 %copy-start.43 = (bf16[256,512]{0,1:T(8,128)(2,1)}, bf16[256,512]{0,1:T(8,128)(2,1)S(1)}, u32[]{:S(2)}) copy-start(bf16[256,512]{0,1:T(8,128)(2,1)S(1)} %copy.85) | copy-start | bytes 786436
  46.7 14.9 %copy-start.18 = (f32[8,256,1024]{2,1,0:T(8,128)}, f32[8,256,1024]{2,1,0:T(8,128)S(1)}, u32[]{:S(2)}) copy-start(f32[8,256,1024]{2,1,0:T(8,128)S(1)} %get-tuple-element.174) | copy-start | bytes 25165828
  74.9 5.0 %copy-start.51 = (bf16[1,1024,512]{1,2,0:T(8,128)(2,1)S(1)}, bf16[1,1024,512]{1,2,0:T(8,128)(2,1)}, u32[]{:S(2)}) copy-start(bf16[1,1024,512]{1,2,0:T(8,128)(2,1)} %copy.89) | copy-start | bytes 3145732
  79.9 6.2 %copy-start.35 = (f32[8,1024,256]{1,2,0:T(8,128)S(1)}, f32[8,1024,256]{1,2,0:T(8,128)}, u32[]{:S(2)}) copy-start(f32[8,1024,256]{1,2,0:T(8,128)} %get-tuple-element.176) | copy-start | bytes 25165828
  79.9 6.2 %copy-start.49 = (bf16[1,1024,512]{1,2,0:T(8,128)(2,1)S(1)}, bf16[1,1024,512]{1,2,0:T(8,128)(2,1)}, u32[]{:S(2)}) copy-start(bf16[1,1024,512]{1,2,0:T(8,128)(2,1)} %copy.93) | copy-start | bytes 3145732
  88.4 277.6 %all-reduce.5.cloned.1.call-start = ((), (), s32[]{:S(2)}) async-start(), calls=%async_computation | async-start | bytes 2097152 | tf_op jit(solution)/shard_map/psum | solution.py:131
  89.3 2.0 copy-start
  104.0 4.6 %copy-start.3 = (f32[8,256,256]{2,1,0:T(8,128)S(1)}, f32[8,256,256]{2,1,0:T(8,128)}, u32[]{:S(2)}) copy-start(f32[8,256,256]{2,1,0:T(8,128)} %online-softmax) | copy-start | bytes 6291460
  108.6 2.3 copy-start.19
  108.6 3.6 copy-start.1
  110.9 1.3 copy-start.45
  126.1 4.6 %copy-start.5 = (f32[8,256,256]{2,1,0:T(8,128)S(1)}, f32[8,256,256]{2,1,0:T(8,128)}, u32[]{:S(2)}) copy-start(f32[8,256,256]{2,1,0:T(8,128)} %online-softmax.1) | copy-start | bytes 6291460
  130.7 2.3 copy-start.21
  130.7 3.6 copy-start.16
  133.0 1.3 copy-start.23
  146.4 4.6 %copy-start.7 = (f32[8,256,256]{2,1,0:T(8,128)S(1)}, f32[8,256,256]{2,1,0:T(8,128)}, u32[]{:S(2)}) copy-start(f32[8,256,256]{2,1,0:T(8,128)} %online-softmax.2) | copy-start | bytes 6291460
  151.0 2.3 copy-start.25
  151.0 3.7 copy-start.10
  153.3 1.4 copy-start.27
  166.5 6.1 %copy-start.9 = (f32[8,256,256]{2,1,0:T(8,128)S(1)}, f32[8,256,256]{2,1,0:T(8,128)}, u32[]{:S(2)}) copy-start(f32[8,256,256]{2,1,0:T(8,128)} %online-softmax.3) | copy-start | bytes 6291460
  172.6 5.3 %copy-start.12 = (f32[8,256,256]{2,1,0:T(8,128)S(1)}, f32[8,256,256]{2,1,0:T(8,128)}, u32[]{:S(2)}) copy-start(f32[8,256,256]{2,1,0:T(8,128)} %fusion.125) | copy-start | bytes 6291460
  176.6 1.3 copy-start.30
  181.4 3.9 %copy-start.32 = (f32[8,256,256]{2,1,0:T(8,128)S(1)}, f32[8,256,256]{2,1,0:T(8,128)}, u32[]{:S(2)}) copy-start(f32[8,256,256]{2,1,0:T(8,128)} %fusion.84) | copy-start | bytes 6291460
  181.4 4.0 %copy-start.38 = (f32[256,8,64]{0,2,1:T(8,128)S(1)}, f32[256,8,64]{0,2,1:T(8,128)}, u32[]{:S(2)}) copy-start(f32[256,8,64]{0,2,1:T(8,128)} %get-tuple-element.161) | copy-start | bytes 1572868
  185.4 2.6 copy-start.48
  188.0 7.8 %slice-start = ((s8[8388608]{0:T(1024)(128)(4,1)}), s8[4194304]{0:T(1024)(128)(4,1)S(1)}, s32[]{:S(2)}) async-start(s8[8388608]{0:T(1024)(128)(4,1)} %bitcast.271), calls=%async_computation.2 | async-start | bytes 8388608
  189.9 5.9 %slice-start.1 = ((s8[8388608]{0:T(1024)(128)(4,1)}), s8[4194304]{0:T(1024)(128)(4,1)S(1)}, s32[]{:S(2)}) async-start(s8[8388608]{0:T(1024)(128)(4,1)} %bitcast.271), calls=%async_computation.3 | async-start | bytes 8388608
  189.9 5.9 %copy-start.52 = (bf16[1,1024,512]{1,2,0:T(8,128)(2,1)S(1)}, bf16[1,1024,512]{1,2,0:T(8,128)(2,1)}, u32[]{:S(2)}) copy-start(bf16[1,1024,512]{1,2,0:T(8,128)(2,1)} %copy.89) | copy-start | bytes 3145732
  195.8 3.4 copy-start.34
  201.5 2.3 copy-start.13
  203.7 3.5 copy-start.29
  219.2 3.5 copy-start.2
  222.7 4.4 %copy-start.31 = (f32[8,256,256]{2,1,0:T(8,128)S(1)}, f32[8,256,256]{2,1,0:T(8,128)}, u32[]{:S(2)}) copy-start(f32[8,256,256]{2,1,0:T(8,128)} %copy-done.30) | copy-start | bytes 6291460
  227.1 2.4 copy-start.28
  229.5 2.2 copy-start.11
  231.7 3.5 copy-start.26
  235.2 2.3 copy-start.8
  250.6 4.4 %copy-start.24 = (f32[8,256,256]{2,1,0:T(8,128)S(1)}, f32[8,256,256]{2,1,0:T(8,128)}, u32[]{:S(2)}) copy-start(f32[8,256,256]{2,1,0:T(8,128)} %copy-done.23) | copy-start | bytes 6291460
  255.0 2.2 copy-start.17
  257.2 3.5 copy-start.22
  260.7 2.3 copy-start.6
  280.2 3.2 copy-start.20
  283.4 2.2 copy-start.4
  289.2 11.3 %slice-start.2 = ((s8[8388608]{0:T(1024)(128)(4,1)}), s8[4194304]{0:T(1024)(128)(4,1)S(1)}, s32[]{:S(2)}) async-start(s8[8388608]{0:T(1024)(128)(4,1)} %bitcast.277), calls=%async_computation.4 | async-start | bytes 8388608
  291.4 9.0 %slice-start.3 = ((s8[8388608]{0:T(1024)(128)(4,1)}), s8[4194304]{0:T(1024)(128)(4,1)S(1)}, s32[]{:S(2)}) async-start(s8[8388608]{0:T(1024)(128)(4,1)} %bitcast.277), calls=%async_computation.5 | async-start | bytes 8388608
  294.9 5.5 %copy-start.47 = (f32[8,256,256]{2,1,0:T(8,128)}, f32[8,256,256]{2,1,0:T(8,128)S(1)}, u32[]{:S(2)}) copy-start(f32[8,256,256]{2,1,0:T(8,128)S(1)} %negate_add_fusion) | copy-start | bytes 6291460
  294.9 5.5 %copy-start.50 = (bf16[1,1024,512]{1,2,0:T(8,128)(2,1)S(1)}, bf16[1,1024,512]{1,2,0:T(8,128)(2,1)}, u32[]{:S(2)}) copy-start(bf16[1,1024,512]{1,2,0:T(8,128)(2,1)} %copy.93) | copy-start | bytes 3145732
  302.1 2.6 copy-start.42
  304.6 2.4 copy-start.14
  304.6 3.1 copy-start.46
  304.7 3.9 %copy-start.53 = (f32[8,256,256]{1,2,0:T(8,128)S(1)}, f32[8,256,256]{1,2,0:T(8,128)}, u32[]{:S(2)}) copy-start(f32[8,256,256]{1,2,0:T(8,128)} %fusion.212) | copy-start | bytes 6291460
  312.7 8.0 %copy-start.15 = (bf16[8,1024,256]{1,2,0:T(8,128)(2,1)S(1)}, bf16[8,1024,256]{1,2,0:T(8,128)(2,1)}, u32[]{:S(2)}) copy-start(bf16[8,1024,256]{1,2,0:T(8,128)(2,1)} %copy-done.14) | copy-start | bytes 12582916
  312.8 8.0 %copy-start.44 = (bf16[256,512]{0,1:T(8,128)(2,1)S(1)}, bf16[256,512]{0,1:T(8,128)(2,1)}, u32[]{:S(2)}) copy-start(bf16[256,512]{0,1:T(8,128)(2,1)} %copy-done.43) | copy-start | bytes 786436
  331.0 4.0 %copy-start.54 = (f32[1,8,256,256]{3,2,1,0:T(8,128)S(1)}, f32[1,8,256,256]{3,2,1,0:T(8,128)}, u32[]{:S(2)}) copy-start(f32[1,8,256,256]{3,2,1,0:T(8,128)} %get-tuple-element.184) | copy-start | bytes 6291460
  367.3 1.8 copy-start.37
  370.4 1.6 copy-start.36
Sparse Core Ops, SparseCore 0:
  88.5 53.1 all-reduce.6
  312.9 53.1 all-reduce.4
where the time goes:
time: 388 us; the launch traced here: 380 us
  matrix products  205 us (53%)
  blocking collectives  56.5 us (15%)
  Pallas kernels  33.2 us (9%)
  waiting for transfers between devices  28.7 us (7%)
  local copies, waits for them, and re-layouts  27.3 us (7%)
  between operations  15.4 us (4%)
  other arithmetic  14.3 us (4%)
    dot_general x12, matrix products, newton(): jnp.matmul(product, 7.0 * identity - product, precision=lax.Precision.HIG...  43.2 us
    dot_general x12, matrix products, newton(): jnp.matmul(approx, 13.0 * identity - inner, precision=lax.Precision.HIGHEST)  40.5 us
    dot_general x8, matrix products, newton(): product = jnp.matmul(matrix, approx, precision=lax.Precision.HIGHEST)  36.9 us
    dot_general x12, matrix products, newton(): jnp.matmul(product, 15.0 * identity - inner, precision=lax.Precision.HIGH...  34.1 us
    unnamed x4, Pallas kernels  33.2 us
    psum x1, waiting for transfers between devices, per_device(): total_q, total_k = lax.psum((query_part, key_part), 'seq')  28.7 us
    all_gather x2, blocking collectives, joined(): everything = jax.tree.map(lambda part: lax.all_gather(part, axis), x)  26.2 us
    unnamed x123, local copies, waits for them, and re-layouts  17.6 us
  transfers between devices with their start and end apart: 2, of which 1 were waited for; matrix products, arithmetic and copies ran while one was open for 21% of the time, Pallas kernels for 9%

commit v1 on v0

v1 whole, which is shorter than its diff:
```python
import functools
import math

import jax
import jax.numpy as jnp
from jax import lax
from jax.experimental import pallas as pl
from jax.experimental.pallas import tpu as pltpu
from jax.sharding import PartitionSpec as P

DH = 64
M = 256
ITERS = 4
PAIR = 2 * DH
TEMPER = DH ** (-0.5)
LOG2 = TEMPER * math.log2(math.e)
F32, BF16 = jnp.float32, jnp.bfloat16
HIGH = lax.Precision.HIGH
VMEM_LIMIT = 56 * 1024 * 1024


def mm(a, b, prec=None):
    return lax.dot_general(a, b, (((1,), (0,)), ((), ())), precision=prec, preferred_element_type=F32)


def nt(a, b, prec=None):
    return lax.dot_general(a, b, (((1,), (1,)), ((), ())), precision=prec, preferred_element_type=F32)


def tn(a, b, prec=None):
    return lax.dot_general(a, b, (((0,), (0,)), ((), ())), precision=prec, preferred_element_type=F32)


def own_half(shape, head):
    lane = lax.broadcasted_iota(jnp.int32, shape, len(shape) - 1)
    return lane < DH if head == 0 else lane >= DH


def only(x, head):
    return jnp.where(own_half(x.shape, head), x, jnp.zeros_like(x))


def stacked(x):
    return jnp.concatenate([only(x, 0), only(x, 1)], axis=0)


def halves(x):
    return jnp.where(own_half((M, PAIR), 0), x[:M], x[M:])


def landmark_kernel(q_ref, k_ref, out_ref):
    rows = q_ref.shape[0]
    land = out_ref.shape[1]
    seg = rows // land
    spot = lax.broadcasted_iota(jnp.int32, (land, rows), 0)
    place = lax.broadcasted_iota(jnp.int32, (land, rows), 1)
    member = jnp.where((place >= spot * seg) & (place < spot * seg + seg), 1.0, 0.0).astype(BF16)
    out_ref[0] = (mm(member, q_ref[...]) / seg).astype(BF16)
    out_ref[1] = (mm(member, k_ref[...]) / seg).astype(BF16)


def first_kernel(q_ref, k_ref, v_ref, g_ref, land_ref, wf_ref, eb_ref, mix_ref, comb_ref, stat_ref):
    lq, lk = stacked(land_ref[0]), stacked(land_ref[1])
    rows = q_ref.shape[0]
    for h in range(2):
        sf = nt(lk[h * M : (h + 1) * M], q_ref[...])
        top = jnp.max(sf, axis=0, keepdims=True)
        ef = jnp.exp2((sf - top) * LOG2)
        wf_ref[0, h * M : (h + 1) * M] = (ef * (1.0 / jnp.sum(ef, axis=0, keepdims=True))).astype(BF16)
    comb_ref[0] = halves(mm(wf_ref[0], g_ref[...]))
    tops, mixes = [], []
    for h in range(2):
        sb = nt(lq[h * M : (h + 1) * M], k_ref[...])
        top = jnp.max(sb, axis=1, keepdims=True)
        eb = jnp.exp2((sb - top) * LOG2).astype(BF16)
        eb_ref[0, h * M : (h + 1) * M] = eb
        values = jnp.where(own_half((rows, PAIR), h), v_ref[...], jnp.ones_like(v_ref[...]))
        mixes.append(mm(eb, values))
        tops.append(jnp.broadcast_to(top, (M, PAIR)))
    low = own_half((M, PAIR), 0)
    mix_ref[0] = jnp.where(low, mixes[0], mixes[1])
    total = jnp.where(low, mixes[1], mixes[0])
    tall = jnp.where(low, tops[1], tops[0])
    tall_t, total_t = tall.T, total.T
    stat_ref[0] = jnp.concatenate(
        [tall_t[DH : DH + 1], tall_t[0:1], total_t[DH : DH + 1], total_t[0:1], jnp.zeros((4, M), F32)], axis=0
    )


def forward_kernel(land_ref, soft_ref, x_ref, y_ref, q_ref, inv_ref):
    lq, lk = land_ref[0], land_ref[1]
    rowi = lax.broadcasted_iota(jnp.int32, (M, M), 0)
    coli = lax.broadcasted_iota(jnp.int32, (M, M), 1)
    eye = jnp.where(rowi == coli, 1.0, 0.0)
    soft, scale, xs, prods = [], [], [], []
    for h in range(2):
        s = nt(only(lq, h), lk)
        e = jnp.exp2((s - jnp.max(s, axis=1, keepdims=True)) * LOG2)
        a = e / jnp.sum(e, axis=1, keepdims=True)
        soft_ref[0, h] = a
        inv_s = 1.0 / (jnp.max(jnp.sum(a, axis=0, keepdims=True), axis=1, keepdims=True)
                       * jnp.max(jnp.sum(a, axis=1, keepdims=True), axis=0, keepdims=True))
        soft.append(a)
        scale.append(inv_s)
        xs.append(nt(a, a, HIGH) * inv_s)
        prods.append(None)
    for k in range(ITERS):
        ys = [mm(x, x, HIGH) for x in xs]
        ts = [mm(x, y, HIGH) for x, y in zip(xs, ys)]
        for h in range(2):
            x_ref[0, h, k] = xs[h]
            y_ref[0, h, k] = ys[h]
            q = 3.25 * eye - 3.75 * xs[h] + 1.75 * ys[h] - 0.25 * ts[h]
            q_ref[0, h, k] = q
            prods[h] = q if k == 0 else mm(prods[h], q, HIGH)
            if k < ITERS - 1:
                xs[h] = mm(xs[h], q, HIGH)
    for h in range(2):
        inv_ref[0, h] = tn(soft[h], prods[h], HIGH) * scale[h]


def middle_kernel(parts, dests, mine, mix_ref, comb_ref, stat_ref, inv_ref, full_ref, send_ref):
    low = own_half((M, PAIR), 0)
    stats = []
    for d in range(parts):
        st = stat_ref[d, 0]
        def column(r0, r1):
            wide = jnp.concatenate([jnp.broadcast_to(st[r0 : r0 + 1], (DH, M)), jnp.broadcast_to(st[r1 : r1 + 1], (DH, M))], axis=0)
            return wide.T
        stats.append((column(0, 1), column(2, 3)))
    top = functools.reduce(jnp.maximum, [s[0] for s in stats])
    shrink = [jnp.exp2((s[0] - top) * LOG2) for s in stats]
    total = sum(f * s[1] for f, s in zip(shrink, stats))
    inv_total = 1.0 / total
    mixed = sum(f * mix_ref[d, 0].astype(F32) for d, f in enumerate(shrink)) * inv_total
    gcomb = sum(comb_ref[d, 0].astype(F32) for d in range(parts))
    full_ref[0, 0] = mixed
    full_ref[0, 1] = gcomb
    comb, gm = [], []
    for h in range(2):
        comb.append(mm(inv_ref[0, h], only(mixed, h), HIGH))
        gm.append(tn(inv_ref[0, h], only(gcomb, h), HIGH))
    combined = comb[0] + comb[1]
    gmix = gm[0] + gm[1]
    full_ref[0, 2] = combined
    for i in range(dests):
        if dests == parts:
            factor = shrink[i] * inv_total
        else:
            me = lax.axis_index("seq")
            own = sum(jnp.where(me == d, shrink[d], 0.0) for d in range(parts))
            factor = own * inv_total
        scaled = (gmix * factor).astype(BF16)
        send_ref[i, 0, 0:M] = combined.astype(BF16)
        dot = scaled.astype(F32) * mixed
        for h in range(2):
            rd = -jnp.sum(only(dot, h), axis=1, keepdims=True)
            hi = rd.astype(BF16)
            lo = (rd - hi.astype(F32)).astype(BF16)
            lane = lax.broadcasted_iota(jnp.int32, (M, PAIR), 1)
            start = DH if h == 0 else 0
            zero = jnp.zeros((M, PAIR), BF16)
            rest = jnp.where(lane == start, jnp.broadcast_to(hi, (M, PAIR)), jnp.where(lane == start + 1, jnp.broadcast_to(lo, (M, PAIR)), zero))
            send_ref[i, 0, (1 + h) * M : (2 + h) * M] = jnp.where(own_half((M, PAIR), h), scaled, rest)


def sym(x):
    return 0.5 * (x + x.T)


def backward_kernel(land_ref, soft_ref, x_ref, y_ref, q_ref, full_ref, out_ref):
    mixed, gcomb, combined = full_ref[0, 0], full_ref[0, 1], full_ref[0, 2]
    soft = [soft_ref[0, h] for h in range(2)]
    col = [jnp.sum(a, axis=0, keepdims=True) for a in soft]
    row = [jnp.sum(a, axis=1, keepdims=True) for a in soft]
    cn = [jnp.max(c, axis=1, keepdims=True) for c in col]
    rn = [jnp.max(r, axis=0, keepdims=True) for r in row]
    inv_s = [1.0 / (c * r) for c, r in zip(cn, rn)]
    gc = [only(gcomb, h) for h in range(2)]
    us = [[mm(soft[h], gc[h], HIGH) * inv_s[h]] for h in range(2)]
    ms = [[only(mixed, h)] for h in range(2)]
    for k in range(ITERS - 1):
        for h in range(2):
            us[h].append(mm(q_ref[0, h, k], us[h][-1], HIGH))
            ms[h].append(mm(q_ref[0, h, ITERS - 1 - k], ms[h][-1], HIGH))
    rm = [mm(q_ref[0, h, 0], ms[h][-1], HIGH) for h in range(2)]
    b = [None, None]
    for k in reversed(range(ITERS)):
        xs = [x_ref[0, h, k] for h in range(2)]
        ys = [y_ref[0, h, k] for h in range(2)]
        c = []
        for h in range(2):
            u, m = us[h][k], ms[h][ITERS - 1 - k]
            c.append(0.5 * nt(u + pltpu.roll(m, DH, 1), m + pltpu.roll(u, DH, 1), HIGH))
        t = [-0.25 * c[h] if b[h] is None else 1.75 * b[h] - 0.25 * c[h] for h in range(2)]
        tx = [mm(t[h], xs[h], HIGH) for h in range(2)]
        ty = [mm(t[h], ys[h], HIGH) for h in range(2)]
        for h in range(2):
            if b[h] is None:
                yb = 1.75 * c[h] + sym(tx[h])
                xb = -3.75 * c[h]
            else:
                by = mm(b[h], ys[h], HIGH)
                yb = 1.75 * c[h] - 3.75 * b[h] + sym(tx[h] - 0.5 * by)
                xb = 3.25 * b[h] - 3.75 * c[h]
            b[h] = xb + sym(ty[h] + 2.0 * mm(yb, xs[h], HIGH))
    lq, lk = land_ref[0].astype(F32), land_ref[1].astype(F32)
    qa, ka = [], []
    for h in range(2):
        a = soft[h]
        sbar = -inv_s[h] * (
            jnp.sum(jnp.sum(gc[h] * combined, axis=1, keepdims=True), axis=0, keepdims=True)
            + jnp.sum(jnp.sum(b[h] * x_ref[0, h, 0], axis=1, keepdims=True), axis=0, keepdims=True)
        )
        grad = inv_s[h] * (nt(rm[h], gc[h], HIGH) + 2.0 * mm(b[h], a, HIGH))
        atc = jnp.where(col[h] == cn[h], 1.0, 0.0)
        atr = jnp.where(row[h] == rn[h], 1.0, 0.0)
        grad += atc * (sbar * rn[h] / jnp.sum(atc, axis=1, keepdims=True))
        grad += atr * (sbar * cn[h] / jnp.sum(atr, axis=0, keepdims=True))
        dsa = a * (grad - jnp.sum(grad * a, axis=1, keepdims=True))
        qa.append(mm(dsa, lk, HIGH))
        ka.append(tn(dsa, lq, HIGH))
    low = own_half((M, PAIR), 0)
    out_ref[0, 0] = TEMPER * jnp.where(low, qa[0], qa[1])
    out_ref[0, 1] = TEMPER * jnp.where(low, ka[0], ka[1])


def second_kernel(q_ref, k_ref, v_ref, g_ref, land_ref, wf_ref, eb_ref, got_ref, dq_ref, dk_ref, gv_ref, part_ref):
    lq, lk = stacked(land_ref[0]), stacked(land_ref[1])
    rows = q_ref.shape[0]
    comb = stacked(got_ref[0, 0:M])
    dsf = []
    for h in range(2):
        gf = nt(comb[h * M : (h + 1) * M], g_ref[...])
        w = wf_ref[0, h * M : (h + 1) * M].astype(F32)
        r = jnp.sum(gf * w, axis=0, keepdims=True)
        dsf.append((w * (gf - r)).astype(BF16))
    dsf = jnp.concatenate(dsf, axis=0)
    dq_ref[...] = TEMPER * tn(lk, dsf).T
    part_ref[1] = TEMPER * halves(mm(dsf, q_ref[...]))
    dsb, gms = [], []
    for h in range(2):
        gx = got_ref[0, (1 + h) * M : (2 + h) * M]
        values = jnp.where(own_half((rows, PAIR), h), v_ref[...], jnp.ones_like(v_ref[...]))
        gb = nt(gx, values)
        dsb.append((eb_ref[0, h * M : (h + 1) * M].astype(F32) * gb).astype(BF16))
        gms.append(only(gx, h))
    dsb = jnp.concatenate(dsb, axis=0)
    gms = jnp.concatenate(gms, axis=0)
    gv_ref[...] = tn(gms, eb_ref[0]).T.astype(BF16)
    part_ref[0] = TEMPER * halves(mm(dsb, k_ref[...]))
    dk_ref[...] = TEMPER * tn(lq, dsb).T


def last_kernel(parts, dq_ref, dk_ref, got_ref, gq_ref, gk_ref):
    land = got_ref.shape[2]
    rows = dq_ref.shape[0]
    seg = rows // land
    for i, (src, dst) in enumerate(((dq_ref, gq_ref), (dk_ref, gk_ref))):
        total = sum(got_ref[d, i].astype(F32) for d in range(parts)) / seg
        wide = jnp.broadcast_to(total[:, None, :], (land, seg, PAIR)).reshape(rows, PAIR)
        dst[...] = (src[...] + wide).astype(BF16)


def params():
    return pltpu.CompilerParams(vmem_limit_bytes=VMEM_LIMIT)


def cost(flops, moved):
    return pl.CostEstimate(flops=int(flops), bytes_accessed=int(moved), transcendentals=0)


def shape(dims, dtype=F32):
    return jax.ShapeDtypeStruct(dims, dtype)


def spread_out(x, spread, personal):
    me = lax.axis_index("seq")
    def to(d):
        return lax.dynamic_index_in_dim(x, d, 0, keepdims=False) if personal else x
    got = [to(me)]
    for step in range(1, spread):
        perm = [(i, (i + step) % spread) for i in range(spread)]
        got.append(lax.ppermute(to(lax.rem(me + step, spread)), "seq", perm))
    table = jnp.stack(got)
    return jnp.stack([lax.dynamic_index_in_dim(table, lax.rem(me - s + spread, spread), 0, keepdims=False) for s in range(spread)])


def per_device(query_rows, key_rows, value_rows, grad_output):
    _, rows, width = query_rows.shape
    q, k, v, g = (x[0] for x in (query_rows, key_rows, value_rows, grad_output))
    spread = lax.axis_size("seq")
    me = lax.axis_index("seq")
    land_dev = M // spread
    pairs = width // PAIR
    shared = pairs == spread
    owned = 1 if shared else pairs

    land = pl.pallas_call(landmark_kernel, out_shape=shape((2, land_dev, width), BF16), compiler_params=params())(q, k)
    land = spread_out(land, spread, False)
    land = jnp.swapaxes(land, 0, 1).reshape(2, M, width)

    cols = pl.BlockSpec((rows, PAIR), lambda p: (0, p))
    lands = pl.BlockSpec((2, M, PAIR), lambda p: (0, 0, p))
    def lead(*dims):
        return pl.BlockSpec((1,) + dims, lambda p: (p,) + (0,) * len(dims))
    wf, eb, mix, comb, stat = pl.pallas_call(
        first_kernel,
        grid=(pairs,),
        in_specs=[cols] * 4 + [lands],
        out_specs=[lead(2 * M, rows), lead(2 * M, rows), lead(M, PAIR), lead(M, PAIR), lead(8, M)],
        out_shape=[shape((pairs, 2 * M, rows), BF16), shape((pairs, 2 * M, rows), BF16), shape((pairs, M, PAIR)), shape((pairs, M, PAIR)), shape((pairs, 8, M))],
        compiler_params=params(),
    )(q, k, v, g, land)

    land_own = lax.dynamic_slice_in_dim(land, me * PAIR, PAIR, 2) if shared else land
    squares = lead(2, M, M)
    steps = lead(2, ITERS, M, M)
    soft, xs, ys, qs, inv = pl.pallas_call(
        forward_kernel,
        grid=(owned,),
        in_specs=[lands],
        out_specs=[squares, steps, steps, steps, squares],
        out_shape=[shape((owned, 2, M, M))] + [shape((owned, 2, ITERS, M, M))] * 3 + [shape((owned, 2, M, M))],
        compiler_params=params(),
        cost_estimate=cost(16 * 12 * M**3 * 2 * owned, 8 * 2**20 * owned),
    )(land_own)

    if shared:
        bundle = jnp.concatenate([mix, comb], axis=1).astype(BF16)
        bundle = spread_out(bundle, spread, True)
        stat = spread_out(stat, spread, True)
        mix_all, comb_all, stat_all = bundle[:, None, :M], bundle[:, None, M:], stat[:, None]
    else:
        mix_all, comb_all, stat_all = (lax.all_gather(x, "seq") for x in (mix, comb, stat))
    dests = spread if shared else 1
    full, send = pl.pallas_call(
        functools.partial(middle_kernel, spread, dests, None),
        grid=(owned,),
        in_specs=[
            pl.BlockSpec((spread, 1, M, PAIR), lambda p: (0, p, 0, 0)),
            pl.BlockSpec((spread, 1, M, PAIR), lambda p: (0, p, 0, 0)),
            pl.BlockSpec((spread, 1, 8, M), lambda p: (0, p, 0, 0)),
            squares,
        ],
        out_specs=[lead(3, M, PAIR), pl.BlockSpec((dests, 1, 3 * M, PAIR), lambda p: (0, p, 0, 0))],
        out_shape=[shape((owned, 3, M, PAIR)), shape((dests, owned, 3 * M, PAIR), BF16)],
        compiler_params=params(),
    )(mix_all, comb_all, stat_all, inv)

    land_grads = pl.pallas_call(
        backward_kernel,
        grid=(owned,),
        in_specs=[lands, squares, steps, steps, steps, lead(3, M, PAIR)],
        out_specs=lead(2, M, PAIR),
        out_shape=shape((owned, 2, M, PAIR)),
        compiler_params=params(),
        cost_estimate=cost(24 * 12 * M**3 * 2 * owned, 8 * 2**20 * owned),
    )(land_own, soft, xs, ys, qs, full)

    got = spread_out(send[:, 0], spread, True) if shared else send[0]

    dq, dk, gv, part = pl.pallas_call(
        second_kernel,
        grid=(pairs,),
        in_specs=[cols] * 4 + [lands, lead(2 * M, rows), lead(2 * M, rows), lead(3 * M, PAIR)],
        out_specs=[cols, cols, cols, lands],
        out_shape=[shape((rows, width)), shape((rows, width)), shape((rows, width), BF16), shape((2, M, width))],
        compiler_params=params(),
    )(q, k, v, g, land, wf, eb, got)

    if shared:
        mine = lax.dynamic_slice_in_dim(part, me * PAIR, PAIR, 2) + land_grads[0]
        part = lax.dynamic_update_slice_in_dim(part, mine, me * PAIR, 2)
    else:
        extra = jnp.swapaxes(land_grads, 0, 1).transpose(0, 2, 1, 3).reshape(2, M, width)
        part = part + jnp.where(me == 0, 1.0, 0.0) * extra
    part = part.astype(BF16).reshape(2, spread, land_dev, width).swapaxes(0, 1)
    final = spread_out(part, spread, True)

    gq, gk = pl.pallas_call(
        functools.partial(last_kernel, spread),
        grid=(pairs,),
        in_specs=[cols, cols, pl.BlockSpec((spread, 2, land_dev, PAIR), lambda p: (0, 0, 0, p))],
        out_specs=[cols, cols],
        out_shape=[shape((rows, width), BF16)] * 2,
        compiler_params=params(),
    )(dq, dk, final)
    return gq[None], gk[None], gv[None]


def solution(mesh):
    spec = P(("groups", "batch"), "seq", "head")
    return jax.shard_map(per_device, mesh=mesh, in_specs=(spec,) * 4, out_specs=(spec,) * 3, check_vma=False)
```

time: 388 us -> 118 us (0.30); the launches traced: 380 us -> 118 us
  matrix products: 205 us -> 0 us
  blocking collectives: 56.5 us -> 0 us
  starting transfers between devices: 0.25 us -> 23.9 us
  local copies, waits for them, and re-layouts: 27.3 us -> 3.92 us
  Pallas kernels: 33.2 us -> 53.4 us
  between operations: 15.4 us -> 0.78 us
  other arithmetic: 14.3 us -> 9 us
    dot_general x60 -> x0, matrix products: 200 us -> none  [the longest x12 43.2 us: newton(): jnp.matmul(product, 7.0 * identity - product, precision=lax.Precision.HIG...]
    all_gather x4 -> x0, blocking collectives: 56.5 us -> none  [the longest x2 26.2 us: joined(): everything = jax.tree.map(lambda part: lax.all_gather(part, axis), x)]
    pallas_call x0 -> x7, Pallas kernels: none -> 53.4 us  [the longest x1 13.2 us: per_device(): pl.pallas_call(backward_kernel, grid=(owned,), in_specs=[lands, squares,...]
    unnamed x4 -> x0, Pallas kernels: 33.2 us -> none
    psum x2 -> x0, waiting for transfers between devices: 28.7 us -> none  [the longest x1 28.7 us: per_device(): total_q, total_k = lax.psum((query_part, key_part), 'seq')]
    ppermute x0 -> x15, waiting for transfers between devices: none -> 26.9 us  [spread_out(): got.append(lax.ppermute(to(lax.rem(me + step, spread)), 'seq', perm))]
    ppermute x0 -> x15, starting transfers between devices: none -> 23.9 us  [spread_out(): got.append(lax.ppermute(to(lax.rem(me + step, spread)), 'seq', perm))]
    unnamed x123 -> x4, local copies, waits for them, and re-layouts: 17.6 us -> 0.01 us
  transfers between devices with their start and end apart: 2 -> 15, of which waited for: 1 -> 7; matrix products, arithmetic and copies ran while one was open for 21% -> 2% of each run, Pallas kernels for 9% -> 11%
where the time goes in v1:
time: 118 us
  Pallas kernels  53.4 us (45%)
  waiting for transfers between devices  26.9 us (23%)
  starting transfers between devices  23.9 us (20%)
  other arithmetic  9 us (8%)
  local copies, waits for them, and re-layouts  3.92 us (3%)
    ppermute x15, waiting for transfers between devices, spread_out(): got.append(lax.ppermute(to(lax.rem(me + step, spread)), 'seq', perm))  26.9 us
    ppermute x15, starting transfers between devices, spread_out(): got.append(lax.ppermute(to(lax.rem(me + step, spread)), 'seq', perm))  23.9 us
    pallas_call x1, Pallas kernels, per_device(): pl.pallas_call(backward_kernel, grid=(owned,), in_specs=[lands, squares,...  13.2 us
    pallas_call x1, Pallas kernels, per_device(): pl.pallas_call(second_kernel, grid=(pairs,), in_specs=[cols] * 4 + [lands...  11.6 us
    pallas_call x1, Pallas kernels, per_device(): pl.pallas_call(first_kernel, grid=(pairs,), in_specs=[cols] * 4 + [lands]...  10.7 us
    pallas_call x1, Pallas kernels, per_device(): pl.pallas_call(forward_kernel, grid=(owned,), in_specs=[lands], out_specs...  7.71 us
    pallas_call x1, Pallas kernels, per_device(): pl.pallas_call(functools.partial(last_kernel, spread), grid=(pairs,), in_...  4.26 us
    pallas_call x1, Pallas kernels, per_device(): pl.pallas_call(functools.partial(middle_kernel, spread, dests, None), gri...  3.3 us
  transfers between devices with their start and end apart: 15, of which 7 were waited for; matrix products, arithmetic and copies ran while one was open for 2% of the time, Pallas kernels for 11%

profile of v1, /device:TPU:0, one launch (start us, length us, event | category | flops | bytes accessed | tf_op | source)
XLA Modules:
  0.0 117.9 jit_solution(6641857452792316114)
XLA Ops:
  0.6 2.7 %shard_map.67 = bf16[2,64,512]{2,1,0:T(8,128)(2,1)} custom-call(bf16[1024,512]{1,0:T(8,128)(2,1)} %bitcast.75, bf16[1024,512]{1,0:T(8,128)(2,1)} %bitcast.78), custom_call_target="tpu_custom_call" | custom-call | tf_op jit(solution)/shard_map/pallas_call | solution.py:299
  3.3 5.0 %collective-permute-start.2 = (bf16[2,64,512]{2,1,0:T(8,128)(2,1)}, bf16[2,64,512]{2,1,0:T(8,128)(2,1)S(1)}, u32[]{:S(2)}, u32[]{:S(2)}) collective-permute-start(bf16[2,64,512]{2,1,0:T(8,128)(2,1)} %shard_map.67), channel_id=1, source_target_pairs={{0,12},{4,0},{8,4},{12,8},{1,13},{5,1},{9,5},{13,9},{2,14},{6,2},{... | collective-permute-start | bytes 393224 | tf_op jit(solution)/shard_map/ppermute | solution.py:284
  8.4 0.0 collective-permute-start.1
  8.4 1.0 collective-permute-start
  9.4 3.2 %collective-permute-done.2 = bf16[2,64,512]{2,1,0:T(8,128)(2,1)S(1)} collective-permute-done((bf16[2,64,512]{2,1,0:T(8,128)(2,1)}, bf16[2,64,512]{2,1,0:T(8,128)(2,1)S(1)}, u32[]{:S(2)}, u32[]{:S(2)}) %collective-permute-start.2) | collective-permute-done | bytes 131104 | tf_op jit(solution)/shard_map/ppermute | solution.py:284
  12.6 7.2 %collective-permute-done.1 = bf16[2,64,512]{2,1,0:T(8,128)(2,1)S(1)} collective-permute-done((bf16[2,64,512]{2,1,0:T(8,128)(2,1)}, bf16[2,64,512]{2,1,0:T(8,128)(2,1)S(1)}, u32[]{:S(2)}, u32[]{:S(2)}) %collective-permute-start.1) | collective-permute-done | bytes 131104 | tf_op jit(solution)/shard_map/ppermute | solution.py:284
  19.8 0.0 collective-permute-done
  19.8 1.0 pad_maximum_fusion.2
  20.8 0.1 maximum_bitcast_fusion
  20.9 0.0 copy-start
  20.9 0.7 constant_dynamic-slice_fusion.7.land_ref
  21.7 7.7 %shard_map.69 = (f32[1,2,256,256]{3,2,1,0:T(8,128)}, f32[1,2,4,256,256]{4,3,2,1,0:T(8,128)}, f32[1,2,4,256,256]{4,3,2,1,0:T(8,128)}, f32[1,2,4,256,256]{4,3,2,1,0:T(8,128)}, f32[1,2,256,256]{3,2,1,0:T(8,128)}) custom-call(bf16[2,256,128]{2,1,0:T(8,128)(2,1)} %constant_dynamic-slice_fusion.7.land_ref), custom_call_target="tpu_custom_call" | custom-call | flops 6442450944 | bytes 8388608 | tf_op jit(solution)/shard_map/pallas_call | solution.py:319
  29.4 0.0 copy-done
  29.4 10.7 %shard_map.68 = (bf16[4,512,1024]{2,1,0:T(8,128)(2,1)}, bf16[4,512,1024]{2,1,0:T(8,128)(2,1)}, f32[4,256,128]{2,1,0:T(8,128)}, f32[4,256,128]{2,1,0:T(8,128)}, f32[4,8,256]{2,1,0:T(8,128)}) custom-call(bf16[1024,512]{1,0:T(8,128)(2,1)} %bitcast.76, bf16[1024,512]{1,0:T(8,128)(2,1)} %bitcast.79, bf16[1024,512]{1,0:T(8,128)(2,1)} %bitcast.84, ...), custom_call_target="tpu_custom_call" | custom-call | tf_op jit(solution)/shard_map/pallas_call | solution.py:307
  40.1 0.8 constant_dynamic-slice_fusion.15
  40.8 1.6 %collective-permute-start.8 = (f32[8,256]{1,0:T(8,128)S(1)}, f32[8,256]{1,0:T(8,128)S(1)}, u32[]{:S(2)}, u32[]{:S(2)}) collective-permute-start(f32[8,256]{1,0:T(8,128)S(1)} %get-tuple-element.74), channel_id=1, source_target_pairs={{0,12},{4,0},{8,4},{12,8},{1,13},{5,1},{9,5},{13,9},{2,14},{6,2},{... | collective-permute-start | bytes 24584 | tf_op jit(solution)/shard_map/ppermute | solution.py:284
  42.4 1.1 collective-permute-start.7
  43.5 2.0 %collective-permute-start.6 = (f32[8,256]{1,0:T(8,128)S(1)}, f32[8,256]{1,0:T(8,128)S(1)}, u32[]{:S(2)}, u32[]{:S(2)}) collective-permute-start(f32[8,256]{1,0:T(8,128)S(1)} %get-tuple-element.76), channel_id=1, source_target_pairs={{0,4},{4,8},{8,12},{12,0},{1,5},{5,9},{9,13},{13,1},{2,6},{6,10},{... | collective-permute-start | bytes 24584 | tf_op jit(solution)/shard_map/ppermute | solution.py:284
  45.5 1.1 convert.6
  46.6 1.1 convert.7
  47.7 0.5 collective-permute-start.3
  48.2 2.0 %collective-permute-start.4 = (bf16[512,128]{1,0:T(8,128)(2,1)S(1)}, bf16[512,128]{1,0:T(8,128)(2,1)S(1)}, u32[]{:S(2)}, u32[]{:S(2)}) collective-permute-start(bf16[512,128]{1,0:T(8,128)(2,1)S(1)} %get-tuple-element.63), channel_id=1, source_target_pairs={{0,8},{4,12},{8,0},{12,4},{1,9},{5,13},{9,1},{13,5},{2,10},{6,14},... | collective-permute-start | bytes 393224 | tf_op jit(solution)/shard_map/ppermute | solution.py:284
  50.2 0.0 collective-permute-done.8
  50.2 1.4 %collective-permute-start.5 = (bf16[512,128]{1,0:T(8,128)(2,1)S(1)}, bf16[512,128]{1,0:T(8,128)(2,1)S(1)}, u32[]{:S(2)}, u32[]{:S(2)}) collective-permute-start(bf16[512,128]{1,0:T(8,128)(2,1)S(1)} %get-tuple-element.64), channel_id=1, source_target_pairs={{0,12},{4,0},{8,4},{12,8},{1,13},{5,1},{9,5},{13,9},{2,14},{6,2},{... | collective-permute-start | bytes 393224 | tf_op jit(solution)/shard_map/ppermute | solution.py:284
  51.6 0.0 collective-permute-done.7
  51.6 0.0 collective-permute-done.6
  51.6 0.6 maximum_bitcast_fusion.1.stat_ref
  52.2 3.8 %collective-permute-done.3 = bf16[512,128]{1,0:T(8,128)(2,1)S(1)} collective-permute-done((bf16[512,128]{1,0:T(8,128)(2,1)S(1)}, bf16[512,128]{1,0:T(8,128)(2,1)S(1)}, u32[]{:S(2)}, u32[]{:S(2)}) %collective-permute-start.3) | collective-permute-done | bytes 131104 | tf_op jit(solution)/shard_map/ppermute | solution.py:284
  56.0 3.2 %collective-permute-done.4 = bf16[512,128]{1,0:T(8,128)(2,1)S(1)} collective-permute-done((bf16[512,128]{1,0:T(8,128)(2,1)S(1)}, bf16[512,128]{1,0:T(8,128)(2,1)S(1)}, u32[]{:S(2)}, u32[]{:S(2)}) %collective-permute-start.4) | collective-permute-done | bytes 131104 | tf_op jit(solution)/shard_map/ppermute | solution.py:284
  59.2 0.0 collective-permute-done.5
  59.2 0.1 pad_maximum_fusion.3
  59.3 0.1 pad_maximum_fusion.4
  59.4 0.8 slice_bitcast_fusion
  60.2 3.3 %shard_map.70 = (f32[1,3,256,128]{3,2,1,0:T(8,128)}, bf16[4,1,768,128]{3,2,1,0:T(8,128)(2,1)}) custom-call(bf16[4,1,256,128]{3,2,1,0:T(8,128)(2,1)} %get-tuple-element.56.mix_ref, bf16[4,1,256,128]{3,2,1,0:T(8,128)(2,1)} %get-tuple-element.55.comb_ref, f32[4,1,8,256]{3,2,1,0:T(8,128)} %maximum_bitcast_fusion.1.stat_ref, ...), custom_call_target="tpu_custom_call" | custom-call | tf_op jit(solution)/shard_map/pallas_call | solution.py:337
  63.5 1.3 %dynamic-slice_bitcast_fusion.3 = (bf16[1,768,128]{2,1,0:T(8,128)(2,1)S(1)}, bf16[768,128]{1,0:T(8,128)(2,1)S(1)}, bf16[768,128]{1,0:T(8,128)(2,1)S(1)}, bf16[768,128]{1,0:T(8,128)(2,1)S(1)}) fusion(bf16[4,1,768,128]{3,2,1,0:T(8,128)(2,1)} %get-tuple-element.27, s32[]{:T(128)S(6)} %select_n.59, s32[]{:T(128)S(6)} %select_n.56, s32[]{:T(128)S(6)} %select_n.57, ...), kind=kLoop, calls=%fused_computation.23 | loop fusion | bytes 1572880 | tf_op jit(solution)/shard_map/jit(dynamic_index_in_dim)/dynamic_slice | solution.py:280
  64.8 3.2 %collective-permute-start.11 = (bf16[768,128]{1,0:T(8,128)(2,1)S(1)}, bf16[768,128]{1,0:T(8,128)(2,1)S(1)}, u32[]{:S(2)}, u32[]{:S(2)}) collective-permute-start(bf16[768,128]{1,0:T(8,128)(2,1)S(1)} %get-tuple-element.44), channel_id=1, source_target_pairs={{0,12},{4,0},{8,4},{12,8},{1,13},{5,1},{9,5},{13,9},{2,14},{6,2},{... | collective-permute-start | bytes 589832 | tf_op jit(solution)/shard_map/ppermute | solution.py:284
  68.0 0.7 collective-permute-start.10
  68.7 0.0 collective-permute-start.9
  68.7 13.2 %shard_map.72 = f32[1,2,256,128]{3,2,1,0:T(8,128)} custom-call(bf16[2,256,128]{2,1,0:T(8,128)(2,1)} %constant_dynamic-slice_fusion.7.land_ref, f32[1,2,256,256]{3,2,1,0:T(8,128)} %get-tuple-element.31.soft_ref, f32[1,2,4,256,256]{4,3,2,1,0:T(8,128)} %get-tuple-element.32.x_ref, f32[1,2,4,256,256]{4,3,2,1,0:T(8,128)} %get-tuple-element.33.y_ref, ...), custom_call_target="tpu_custom_call" | custom-call | flops 9663676416 | bytes 8388608 | tf_op jit(solution)/shard_map/pallas_call | solution.py:351
  81.9 0.0 collective-permute-done.11
  81.9 3.4 %collective-permute-done.10 = bf16[768,128]{1,0:T(8,128)(2,1)S(1)} collective-permute-done((bf16[768,128]{1,0:T(8,128)(2,1)S(1)}, bf16[768,128]{1,0:T(8,128)(2,1)S(1)}, u32[]{:S(2)}, u32[]{:S(2)}) %collective-permute-start.10) | collective-permute-done | bytes 196640 | tf_op jit(solution)/shard_map/ppermute | solution.py:284
  85.2 0.0 collective-permute-done.9
  85.2 0.1 pad_maximum_fusion
  85.3 0.1 constant_dynamic-slice_fusion.6
  85.4 1.0 pad_maximum_fusion.1.got_ref
  86.4 0.0 copy-start.1
  86.4 11.6 %shard_map.71 = (f32[1024,512]{1,0:T(8,128)}, f32[1024,512]{1,0:T(8,128)}, bf16[1024,512]{1,0:T(8,128)(2,1)}, f32[2,256,512]{2,1,0:T(8,128)}) custom-call(bf16[1024,512]{1,0:T(8,128)(2,1)} %bitcast.77, bf16[1024,512]{1,0:T(8,128)(2,1)} %bitcast.80, bf16[1024,512]{1,0:T(8,128)(2,1)} %bitcast.85, bf16[1024,512]{1,0:T(8,128)(2,1)} %bitcast.87, ...), custom_call_target="tpu_custom_call" | custom-call | tf_op jit(solution)/shard_map/pallas_call | solution.py:363
  98.0 0.0 copy-done.1
  98.0 1.7 %fusion = f32[2,256,512]{2,1,0:T(8,128)} fusion(f32[2,256,512]{2,1,0:T(8,128)} %get-tuple-element.30, s32[]{:T(128)S(6)} %select_n.60, f32[1,2,256,128]{3,2,1,0:T(8,128)S(1)} %copy-done.1), kind=kLoop, calls=%fused_computation.19 | loop fusion | flops 65536 | bytes 786436 | tf_op jit(solution)/shard_map/dynamic_update_slice | solution.py:374
  99.7 1.3 %convert_element_type.4 = bf16[2,256,512]{2,1,0:T(8,128)(2,1)S(1)} convert(f32[2,256,512]{2,1,0:T(8,128)} %fusion) | non-fusion elementwise | flops 262144 | bytes 1572864 | tf_op jit(solution)/shard_map/convert_element_type | solution.py:378
  101.0 1.6 %collective-permute-start.13 = (bf16[2,64,512]{2,1,0:T(8,128)(2,1)S(1)}, bf16[2,64,512]{2,1,0:T(8,128)(2,1)S(1)}, u32[]{:S(2)}, u32[]{:S(2)}) collective-permute-start(bf16[2,64,512]{2,1,0:T(8,128)(2,1)S(1)} %get-tuple-element.52), channel_id=1, source_target_pairs={{0,8},{4,12},{8,0},{12,4},{1,9},{5,13},{9,1},{13,5},{2,10},{6,14},... | collective-permute-start | bytes 393224 | tf_op jit(solution)/shard_map/ppermute | solution.py:284
  102.6 0.0 collective-permute-start.12
  102.6 3.8 %collective-permute-start.14 = (bf16[2,64,512]{2,1,0:T(8,128)(2,1)S(1)}, bf16[2,64,512]{2,1,0:T(8,128)(2,1)S(1)}, u32[]{:S(2)}, u32[]{:S(2)}) collective-permute-start(bf16[2,64,512]{2,1,0:T(8,128)(2,1)S(1)} %get-tuple-element.54), channel_id=1, source_target_pairs={{0,12},{4,0},{8,4},{12,8},{1,13},{5,1},{9,5},{13,9},{2,14},{6,2},{... | collective-permute-start | bytes 393224 | tf_op jit(solution)/shard_map/ppermute | solution.py:284
  106.4 5.3 %collective-permute-done.13 = bf16[2,64,512]{2,1,0:T(8,128)(2,1)S(1)} collective-permute-done((bf16[2,64,512]{2,1,0:T(8,128)(2,1)S(1)}, bf16[2,64,512]{2,1,0:T(8,128)(2,1)S(1)}, u32[]{:S(2)}, u32[]{:S(2)}) %collective-permute-start.13) | collective-permute-done | bytes 131104 | tf_op jit(solution)/shard_map/ppermute | solution.py:284
  111.7 0.0 collective-permute-done.12
  111.7 0.9 collective-permute-done.14
  112.6 0.1 pad_maximum_fusion.5
  112.7 0.9 pad_maximum_fusion.6.got_ref
  113.6 4.3 %shard_map.73 = (bf16[1024,512]{1,0:T(8,128)(2,1)}, bf16[1024,512]{1,0:T(8,128)(2,1)}) custom-call(f32[1024,512]{1,0:T(8,128)} %get-tuple-element.28.dq_ref, f32[1024,512]{1,0:T(8,128)} %get-tuple-element.29.dk_ref, bf16[4,2,64,512]{3,2,1,0:T(8,128)(2,1)} %pad_maximum_fusion.6.got_ref), custom_call_target="tpu_custom_call" | custom-call | tf_op jit(solution)/shard_map/pallas_call | solution.py:381
  (8 shorter events, 0.3 us)
Async XLA Ops:
  3.3 9.3 %collective-permute-start.2 = (bf16[2,64,512]{2,1,0:T(8,128)(2,1)}, bf16[2,64,512]{2,1,0:T(8,128)(2,1)S(1)}, u32[]{:S(2)}, u32[]{:S(2)}) collective-permute-start(bf16[2,64,512]{2,1,0:T(8,128)(2,1)} %shard_map.67), channel_id=1, source_target_pairs={{0,12},{4,0},{8,4},{12,8},{1,13},{5,1},{9,5},{13,9},{2,14},{6,2},{... | collective-permute-start | bytes 393224 | tf_op jit(solution)/shard_map/ppermute | solution.py:284
  8.4 11.4 %collective-permute-start.1 = (bf16[2,64,512]{2,1,0:T(8,128)(2,1)}, bf16[2,64,512]{2,1,0:T(8,128)(2,1)S(1)}, u32[]{:S(2)}, u32[]{:S(2)}) collective-permute-start(bf16[2,64,512]{2,1,0:T(8,128)(2,1)} %shard_map.67), channel_id=1, source_target_pairs={{0,8},{4,12},{8,0},{12,4},{1,9},{5,13},{9,1},{13,5},{2,10},{6,14},... | collective-permute-start | bytes 393224 | tf_op jit(solution)/shard_map/ppermute | solution.py:284
  8.4 11.4 %collective-permute-start = (bf16[2,64,512]{2,1,0:T(8,128)(2,1)}, bf16[2,64,512]{2,1,0:T(8,128)(2,1)S(1)}, u32[]{:S(2)}, u32[]{:S(2)}) collective-permute-start(bf16[2,64,512]{2,1,0:T(8,128)(2,1)} %shard_map.67), channel_id=1, source_target_pairs={{0,4},{4,8},{8,12},{12,0},{1,5},{5,9},{9,13},{13,1},{2,6},{6,10},{... | collective-permute-start | bytes 393224 | tf_op jit(solution)/shard_map/ppermute | solution.py:284
  20.9 8.5 %copy-start = (bf16[2,4,64,512]{3,2,1,0:T(8,128)(2,1)}, bf16[2,4,64,512]{3,2,1,0:T(8,128)(2,1)S(1)}, u32[]{:S(2)}) copy-start(bf16[2,4,64,512]{3,2,1,0:T(8,128)(2,1)S(1)} %copy.7) | copy-start | bytes 1572868
  40.8 9.3 %collective-permute-start.8 = (f32[8,256]{1,0:T(8,128)S(1)}, f32[8,256]{1,0:T(8,128)S(1)}, u32[]{:S(2)}, u32[]{:S(2)}) collective-permute-start(f32[8,256]{1,0:T(8,128)S(1)} %get-tuple-element.74), channel_id=1, source_target_pairs={{0,12},{4,0},{8,4},{12,8},{1,13},{5,1},{9,5},{13,9},{2,14},{6,2},{... | collective-permute-start | bytes 24584 | tf_op jit(solution)/shard_map/ppermute | solution.py:284
  42.4 9.2 %collective-permute-start.7 = (f32[8,256]{1,0:T(8,128)S(1)}, f32[8,256]{1,0:T(8,128)S(1)}, u32[]{:S(2)}, u32[]{:S(2)}) collective-permute-start(f32[8,256]{1,0:T(8,128)S(1)} %get-tuple-element.75), channel_id=1, source_target_pairs={{0,8},{4,12},{8,0},{12,4},{1,9},{5,13},{9,1},{13,5},{2,10},{6,14},... | collective-permute-start | bytes 24584 | tf_op jit(solution)/shard_map/ppermute | solution.py:284
  43.5 8.1 %collective-permute-start.6 = (f32[8,256]{1,0:T(8,128)S(1)}, f32[8,256]{1,0:T(8,128)S(1)}, u32[]{:S(2)}, u32[]{:S(2)}) collective-permute-start(f32[8,256]{1,0:T(8,128)S(1)} %get-tuple-element.76), channel_id=1, source_target_pairs={{0,4},{4,8},{8,12},{12,0},{1,5},{5,9},{9,13},{13,1},{2,6},{6,10},{... | collective-permute-start | bytes 24584 | tf_op jit(solution)/shard_map/ppermute | solution.py:284
  47.7 8.3 %collective-permute-start.3 = (bf16[512,128]{1,0:T(8,128)(2,1)S(1)}, bf16[512,128]{1,0:T(8,128)(2,1)S(1)}, u32[]{:S(2)}, u32[]{:S(2)}) collective-permute-start(bf16[512,128]{1,0:T(8,128)(2,1)S(1)} %get-tuple-element.62), channel_id=1, source_target_pairs={{0,4},{4,8},{8,12},{12,0},{1,5},{5,9},{9,13},{13,1},{2,6},{6,10},{... | collective-permute-start | bytes 393224 | tf_op jit(solution)/shard_map/ppermute | solution.py:284
  48.2 11.0 %collective-permute-start.4 = (bf16[512,128]{1,0:T(8,128)(2,1)S(1)}, bf16[512,128]{1,0:T(8,128)(2,1)S(1)}, u32[]{:S(2)}, u32[]{:S(2)}) collective-permute-start(bf16[512,128]{1,0:T(8,128)(2,1)S(1)} %get-tuple-element.63), channel_id=1, source_target_pairs={{0,8},{4,12},{8,0},{12,4},{1,9},{5,13},{9,1},{13,5},{2,10},{6,14},... | collective-permute-start | bytes 393224 | tf_op jit(solution)/shard_map/ppermute | solution.py:284
  50.2 9.0 %collective-permute-start.5 = (bf16[512,128]{1,0:T(8,128)(2,1)S(1)}, bf16[512,128]{1,0:T(8,128)(2,1)S(1)}, u32[]{:S(2)}, u32[]{:S(2)}) collective-permute-start(bf16[512,128]{1,0:T(8,128)(2,1)S(1)} %get-tuple-element.64), channel_id=1, source_target_pairs={{0,12},{4,0},{8,4},{12,8},{1,13},{5,1},{9,5},{13,9},{2,14},{6,2},{... | collective-permute-start | bytes 393224 | tf_op jit(solution)/shard_map/ppermute | solution.py:284
  64.8 17.1 %collective-permute-start.11 = (bf16[768,128]{1,0:T(8,128)(2,1)S(1)}, bf16[768,128]{1,0:T(8,128)(2,1)S(1)}, u32[]{:S(2)}, u32[]{:S(2)}) collective-permute-start(bf16[768,128]{1,0:T(8,128)(2,1)S(1)} %get-tuple-element.44), channel_id=1, source_target_pairs={{0,12},{4,0},{8,4},{12,8},{1,13},{5,1},{9,5},{13,9},{2,14},{6,2},{... | collective-permute-start | bytes 589832 | tf_op jit(solution)/shard_map/ppermute | solution.py:284
  68.0 17.2 %collective-permute-start.10 = (bf16[768,128]{1,0:T(8,128)(2,1)S(1)}, bf16[768,128]{1,0:T(8,128)(2,1)S(1)}, u32[]{:S(2)}, u32[]{:S(2)}) collective-permute-start(bf16[768,128]{1,0:T(8,128)(2,1)S(1)} %get-tuple-element.45), channel_id=1, source_target_pairs={{0,8},{4,12},{8,0},{12,4},{1,9},{5,13},{9,1},{13,5},{2,10},{6,14},... | collective-permute-start | bytes 589832 | tf_op jit(solution)/shard_map/ppermute | solution.py:284
  68.7 16.5 %collective-permute-start.9 = (bf16[768,128]{1,0:T(8,128)(2,1)S(1)}, bf16[768,128]{1,0:T(8,128)(2,1)S(1)}, u32[]{:S(2)}, u32[]{:S(2)}) collective-permute-start(bf16[768,128]{1,0:T(8,128)(2,1)S(1)} %get-tuple-element.46), channel_id=1, source_target_pairs={{0,4},{4,8},{8,12},{12,0},{1,5},{5,9},{9,13},{13,1},{2,6},{6,10},{... | collective-permute-start | bytes 589832 | tf_op jit(solution)/shard_map/ppermute | solution.py:284
  86.4 11.6 %copy-start.1 = (f32[1,2,256,128]{3,2,1,0:T(8,128)S(1)}, f32[1,2,256,128]{3,2,1,0:T(8,128)}, u32[]{:S(2)}) copy-start(f32[1,2,256,128]{3,2,1,0:T(8,128)} %shard_map.72) | copy-start | bytes 786436
  101.0 10.7 %collective-permute-start.13 = (bf16[2,64,512]{2,1,0:T(8,128)(2,1)S(1)}, bf16[2,64,512]{2,1,0:T(8,128)(2,1)S(1)}, u32[]{:S(2)}, u32[]{:S(2)}) collective-permute-start(bf16[2,64,512]{2,1,0:T(8,128)(2,1)S(1)} %get-tuple-element.52), channel_id=1, source_target_pairs={{0,8},{4,12},{8,0},{12,4},{1,9},{5,13},{9,1},{13,5},{2,10},{6,14},... | collective-permute-start | bytes 393224 | tf_op jit(solution)/shard_map/ppermute | solution.py:284
  102.6 9.1 %collective-permute-start.12 = (bf16[2,64,512]{2,1,0:T(8,128)(2,1)S(1)}, bf16[2,64,512]{2,1,0:T(8,128)(2,1)S(1)}, u32[]{:S(2)}, u32[]{:S(2)}) collective-permute-start(bf16[2,64,512]{2,1,0:T(8,128)(2,1)S(1)} %get-tuple-element.53), channel_id=1, source_target_pairs={{0,4},{4,8},{8,12},{12,0},{1,5},{5,9},{9,13},{13,1},{2,6},{6,10},{... | collective-permute-start | bytes 393224 | tf_op jit(solution)/shard_map/ppermute | solution.py:284
  102.6 10.0 %collective-permute-start.14 = (bf16[2,64,512]{2,1,0:T(8,128)(2,1)S(1)}, bf16[2,64,512]{2,1,0:T(8,128)(2,1)S(1)}, u32[]{:S(2)}, u32[]{:S(2)}) collective-permute-start(bf16[2,64,512]{2,1,0:T(8,128)(2,1)S(1)} %get-tuple-element.54), channel_id=1, source_target_pairs={{0,12},{4,0},{8,4},{12,8},{1,13},{5,1},{9,5},{13,9},{2,14},{6,2},{... | collective-permute-start | bytes 393224 | tf_op jit(solution)/shard_map/ppermute | solution.py:284

commit v2 on v1

--- a/solution.py
+++ b/solution.py
@@ -67,7 +67,7 @@
         top = jnp.max(sf, axis=0, keepdims=True)
         ef = jnp.exp2((sf - top) * LOG2)
         wf_ref[0, h * M : (h + 1) * M] = (ef * (1.0 / jnp.sum(ef, axis=0, keepdims=True))).astype(BF16)
-    comb_ref[0] = halves(mm(wf_ref[0], g_ref[...]))
+    comb_ref[0] = halves(mm(wf_ref[0], g_ref[...])).astype(comb_ref.dtype)
     tops, mixes = [], []
     for h in range(2):
         sb = nt(lq[h * M : (h + 1) * M], k_ref[...])
@@ -78,7 +78,7 @@
         mixes.append(mm(eb, values))
         tops.append(jnp.broadcast_to(top, (M, PAIR)))
     low = own_half((M, PAIR), 0)
-    mix_ref[0] = jnp.where(low, mixes[0], mixes[1])
+    mix_ref[0] = jnp.where(low, mixes[0], mixes[1]).astype(mix_ref.dtype)
     total = jnp.where(low, mixes[1], mixes[0])
     tall = jnp.where(low, tops[1], tops[0])
     tall_t, total_t = tall.T, total.T
@@ -119,11 +119,10 @@
         inv_ref[0, h] = tn(soft[h], prods[h], HIGH) * scale[h]
 
 
-def middle_kernel(parts, dests, mine, mix_ref, comb_ref, stat_ref, inv_ref, full_ref, send_ref):
-    low = own_half((M, PAIR), 0)
+def middle(parts, dests, mixes, combs, stats_in, inv_ref, full_ref, send, send_stat):
     stats = []
     for d in range(parts):
-        st = stat_ref[d, 0]
+        st = stats_in[d]
         def column(r0, r1):
             wide = jnp.concatenate([jnp.broadcast_to(st[r0 : r0 + 1], (DH, M)), jnp.broadcast_to(st[r1 : r1 + 1], (DH, M))], axis=0)
             return wide.T
@@ -132,8 +131,8 @@
     shrink = [jnp.exp2((s[0] - top) * LOG2) for s in stats]
     total = sum(f * s[1] for f, s in zip(shrink, stats))
     inv_total = 1.0 / total
-    mixed = sum(f * mix_ref[d, 0].astype(F32) for d, f in enumerate(shrink)) * inv_total
-    gcomb = sum(comb_ref[d, 0].astype(F32) for d in range(parts))
+    mixed = sum(f * mixes[d].astype(F32) for d, f in enumerate(shrink)) * inv_total
+    gcomb = sum(combs[d].astype(F32) for d in range(parts))
     full_ref[0, 0] = mixed
     full_ref[0, 1] = gcomb
     comb, gm = [], []
@@ -148,20 +147,26 @@
             factor = shrink[i] * inv_total
         else:
             me = lax.axis_index("seq")
-            own = sum(jnp.where(me == d, shrink[d], 0.0) for d in range(parts))
-            factor = own * inv_total
+            factor = sum(jnp.where(me == d, shrink[d], 0.0) for d in range(parts)) * inv_total
         scaled = (gmix * factor).astype(BF16)
-        send_ref[i, 0, 0:M] = combined.astype(BF16)
         dot = scaled.astype(F32) * mixed
-        for h in range(2):
-            rd = -jnp.sum(only(dot, h), axis=1, keepdims=True)
-            hi = rd.astype(BF16)
-            lo = (rd - hi.astype(F32)).astype(BF16)
-            lane = lax.broadcasted_iota(jnp.int32, (M, PAIR), 1)
-            start = DH if h == 0 else 0
-            zero = jnp.zeros((M, PAIR), BF16)
-            rest = jnp.where(lane == start, jnp.broadcast_to(hi, (M, PAIR)), jnp.where(lane == start + 1, jnp.broadcast_to(lo, (M, PAIR)), zero))
-            send_ref[i, 0, (1 + h) * M : (2 + h) * M] = jnp.where(own_half((M, PAIR), h), scaled, rest)
+        rd = [-jnp.sum(only(dot, h), axis=1, keepdims=True) for h in range(2)]
+        low = own_half((M, PAIR), 0)
+        wide = jnp.where(low, jnp.broadcast_to(rd[0], (M, PAIR)), jnp.broadcast_to(rd[1], (M, PAIR))).T
+        send(i, combined.astype(BF16), scaled)
+        send_stat(i, jnp.concatenate([wide[0:1], wide[DH : DH + 1], jnp.zeros((6, M), F32)], axis=0))
+
+
+def middle_kernel(parts, mix_ref, comb_ref, stat_ref, inv_ref, full_ref, send_ref, rd_ref):
+    def send(i, combined, scaled):
+        send_ref[0, :M] = combined
+        send_ref[0, M:] = scaled
+
+    def send_stat(i, rd):
+        rd_ref[0] = rd
+
+    each = range(parts)
+    middle(parts, 1, [mix_ref[d, 0] for d in each], [comb_ref[d, 0] for d in each], [stat_ref[d, 0] for d in each], inv_ref, full_ref, send, send_stat)
 
 
 def sym(x):
@@ -225,7 +230,7 @@
     out_ref[0, 1] = TEMPER * jnp.where(low, ka[0], ka[1])
 
 
-def second_kernel(q_ref, k_ref, v_ref, g_ref, land_ref, wf_ref, eb_ref, got_ref, dq_ref, dk_ref, gv_ref, part_ref):
+def second_kernel(q_ref, k_ref, v_ref, g_ref, land_ref, wf_ref, eb_ref, got_ref, rd_ref, dq_ref, dk_ref, gv_ref, part_ref):
     lq, lk = stacked(land_ref[0]), stacked(land_ref[1])
     rows = q_ref.shape[0]
     comb = stacked(got_ref[0, 0:M])
@@ -240,7 +245,14 @@
     part_ref[1] = TEMPER * halves(mm(dsf, q_ref[...]))
     dsb, gms = [], []
     for h in range(2):
-        gx = got_ref[0, (1 + h) * M : (2 + h) * M]
+        st = rd_ref[0]
+        rd = jnp.broadcast_to(st[h : h + 1], (PAIR, M)).T
+        hi = rd.astype(BF16)
+        lo = (rd - hi.astype(F32)).astype(BF16)
+        lane = lax.broadcasted_iota(jnp.int32, (M, PAIR), 1)
+        start = DH if h == 0 else 0
+        rest = jnp.where(lane == start, hi, jnp.where(lane == start + 1, lo, jnp.zeros_like(hi)))
+        gx = jnp.where(own_half((M, PAIR), h), got_ref[0, M : 2 * M], rest)
         values = jnp.where(own_half((rows, PAIR), h), v_ref[...], jnp.ones_like(v_ref[...]))
         gb = nt(gx, values)
         dsb.append((eb_ref[0, h * M : (h + 1) * M].astype(F32) * gb).astype(BF16))
@@ -286,15 +298,13 @@
     return jnp.stack([lax.dynamic_index_in_dim(table, lax.rem(me - s + spread, spread), 0, keepdims=False) for s in range(spread)])
 
 
-def per_device(query_rows, key_rows, value_rows, grad_output):
-    _, rows, width = query_rows.shape
-    q, k, v, g = (x[0] for x in (query_rows, key_rows, value_rows, grad_output))
+def general(q, k, v, g):
+    rows, width = q.shape
     spread = lax.axis_size("seq")
     me = lax.axis_index("seq")
     land_dev = M // spread
     pairs = width // PAIR
-    shared = pairs == spread
-    owned = 1 if shared else pairs
+    owned = pairs
 
     land = pl.pallas_call(landmark_kernel, out_shape=shape((2, land_dev, width), BF16), compiler_params=params())(q, k)
     land = spread_out(land, spread, False)
@@ -313,7 +323,7 @@
         compiler_params=params(),
     )(q, k, v, g, land)
 
-    land_own = lax.dynamic_slice_in_dim(land, me * PAIR, PAIR, 2) if shared else land
+    land_own = land
     squares = lead(2, M, M)
     steps = lead(2, ITERS, M, M)
     soft, xs, ys, qs, inv = pl.pallas_call(
@@ -326,16 +336,9 @@
         cost_estimate=cost(16 * 12 * M**3 * 2 * owned, 8 * 2**20 * owned),
     )(land_own)
 
-    if shared:
-        bundle = jnp.concatenate([mix, comb], axis=1).astype(BF16)
-        bundle = spread_out(bundle, spread, True)
-        stat = spread_out(stat, spread, True)
-        mix_all, comb_all, stat_all = bundle[:, None, :M], bundle[:, None, M:], stat[:, None]
-    else:
-        mix_all, comb_all, stat_all = (lax.all_gather(x, "seq") for x in (mix, comb, stat))
-    dests = spread if shared else 1
-    full, send = pl.pallas_call(
-        functools.partial(middle_kernel, spread, dests, None),
+    mix_all, comb_all, stat_all = (lax.all_gather(x, "seq") for x in (mix, comb, stat))
+    full, got, rd = pl.pallas_call(
+        functools.partial(middle_kernel, spread),
         grid=(owned,),
         in_specs=[
             pl.BlockSpec((spread, 1, M, PAIR), lambda p: (0, p, 0, 0)),
@@ -343,8 +346,8 @@
             pl.BlockSpec((spread, 1, 8, M), lambda p: (0, p, 0, 0)),
             squares,
         ],
-        out_specs=[lead(3, M, PAIR), pl.BlockSpec((dests, 1, 3 * M, PAIR), lambda p: (0, p, 0, 0))],
-        out_shape=[shape((owned, 3, M, PAIR)), shape((dests, owned, 3 * M, PAIR), BF16)],
+        out_specs=[lead(3, M, PAIR), lead(2 * M, PAIR), lead(8, M)],
+        out_shape=[shape((owned, 3, M, PAIR)), shape((owned, 2 * M, PAIR), BF16), shape((owned, 8, M))],
         compiler_params=params(),
     )(mix_all, comb_all, stat_all, inv)
 
@@ -358,23 +361,17 @@
         cost_estimate=cost(24 * 12 * M**3 * 2 * owned, 8 * 2**20 * owned),
     )(land_own, soft, xs, ys, qs, full)
 
-    got = spread_out(send[:, 0], spread, True) if shared else send[0]
-
     dq, dk, gv, part = pl.pallas_call(
         second_kernel,
         grid=(pairs,),
-        in_specs=[cols] * 4 + [lands, lead(2 * M, rows), lead(2 * M, rows), lead(3 * M, PAIR)],
+        in_specs=[cols] * 4 + [lands, lead(2 * M, rows), lead(2 * M, rows), lead(2 * M, PAIR), lead(8, M)],
         out_specs=[cols, cols, cols, lands],
         out_shape=[shape((rows, width)), shape((rows, width)), shape((rows, width), BF16), shape((2, M, width))],
         compiler_params=params(),
-    )(q, k, v, g, land, wf, eb, got)
-
-    if shared:
-        mine = lax.dynamic_slice_in_dim(part, me * PAIR, PAIR, 2) + land_grads[0]
-        part = lax.dynamic_update_slice_in_dim(part, mine, me * PAIR, 2)
-    else:
-        extra = jnp.swapaxes(land_grads, 0, 1).transpose(0, 2, 1, 3).reshape(2, M, width)
-        part = part + jnp.where(me == 0, 1.0, 0.0) * extra
+    )(q, k, v, g, land, wf, eb, got, rd)
+
+    extra = jnp.swapaxes(land_grads, 0, 1).transpose(0, 2, 1, 3).reshape(2, M, width)
+    part = part + jnp.where(me == 0, 1.0, 0.0) * extra
     part = part.astype(BF16).reshape(2, spread, land_dev, width).swapaxes(0, 1)
     final = spread_out(part, spread, True)
 
@@ -386,7 +383,213 @@
         out_shape=[shape((rows, width), BF16)] * 2,
         compiler_params=params(),
     )(dq, dk, final)
-    return gq[None], gk[None], gv[None]
+    return gq, gk, gv
+
+
+def whole_kernel(
+    spread, q_ref, k_ref, v_ref, g_ref, gq_ref, gk_ref, gv_ref,
+    own_land, land, wf, eb, bsend, ssend, brecv, srecv, soft, xs, ys, qs, inv, full, back, rback, got, rgot,
+    extra, dq, dk, part, psend, fbuf,
+    land_s, land_r, b_s, b_r, s_s, s_r, g_s, g_r, r_s, r_r, f_s, f_r,
+):
+    S = spread
+    me = lax.axis_index("seq")
+    others = range(1, S)
+    land_dev = M // S
+
+    def shift(n):
+        return lax.rem(me + n, S)
+
+    def lanes(p):
+        return pl.ds(pl.multiple_of(p * PAIR, PAIR), PAIR)
+
+    def remote(src, dst, send_sem, recv_sem, to):
+        return pltpu.make_async_remote_copy(
+            src_ref=src, dst_ref=dst, send_sem=send_sem, recv_sem=recv_sem,
+            device_id={"seq": to}, device_id_type=pl.DeviceIdType.MESH,
+        )
+
+    barrier = pltpu.get_barrier_semaphore()
+    for s in others:
+        pl.semaphore_signal(barrier, inc=1, device_id={"seq": shift(s)}, device_id_type=pl.DeviceIdType.MESH)
+
+    landmark_kernel(q_ref, k_ref, own_land)
+    for p in range(S):
+        for i in range(2):
+            land[p, me, i] = own_land[i, :, p * PAIR : (p + 1) * PAIR]
+    pl.semaphore_wait(barrier, S - 1)
+
+    def land_copy(i, s):
+        p = shift(s + 1 + i)
+        return remote(land.at[p, me], land.at[p, me], land_s.at[i, s - 1], land_r.at[i, s - 1], shift(s))
+
+    for i in range(S):
+        for s in others:
+            land_copy(i, s).start()
+
+    def lands(p):
+        both = land[p]
+        return both[:, 0].reshape(M, PAIR), both[:, 1].reshape(M, PAIR)
+
+    def bundle_copy(i):
+        return remote(bsend.at[i], brecv.at[i], b_s.at[i], b_r.at[i], shift(i + 1))
+
+    def stat_copy(i):
+        return remote(ssend.at[i], srecv.at[i], s_s.at[i], s_r.at[i], shift(i + 1))
+
+    def first(i, carry):
+        for s in others:
+            land_copy(i, s).wait_recv()
+        p = shift(i + 1)
+        cols = lanes(p)
+        first_kernel(
+            q_ref.at[:, cols], k_ref.at[:, cols], v_ref.at[:, cols], g_ref.at[:, cols], lands(p),
+            wf.at[pl.ds(p, 1)], eb.at[pl.ds(p, 1)],
+            bsend.at[pl.ds(i, 1), 0:M], bsend.at[pl.ds(i, 1), M : 2 * M], ssend.at[pl.ds(i, 1)],
+        )
+
+        @pl.when(i < S - 1)
+        def _():
+            bundle_copy(i).start()
+            stat_copy(i).start()
+
+        return carry
+
+    lax.fori_loop(0, S, first, 0)
+    land_own = lands(me)
+    forward_kernel(land_own, soft, xs, ys, qs, inv)
+    for i in range(S - 1):
+        bundle_copy(i).wait_recv()
+        stat_copy(i).wait_recv()
+
+    mixes = [bsend[S - 1, 0:M]] + [brecv[i, 0:M] for i in range(S - 1)]
+    combs = [bsend[S - 1, M : 2 * M]] + [brecv[i, M : 2 * M] for i in range(S - 1)]
+    stats = [ssend[S - 1]] + [srecv[i] for i in range(S - 1)]
+
+    def back_copy(s):
+        return remote(back.at[s - 1], got.at[me], g_s.at[s - 1], g_r.at[s - 1], shift(S - s))
+
+    def rback_copy(s):
+        return remote(rback.at[s - 1], rgot.at[me], r_s.at[s - 1], r_r.at[s - 1], shift(S - s))
+
+    def send(s, combined, scaled):
+        if s == 0:
+            got[me, 0:M] = combined
+            got[me, M : 2 * M] = scaled
+        else:
+            back[s - 1, 0:M] = combined
+            back[s - 1, M : 2 * M] = scaled
+            back_copy(s).start()
+
+    def send_stat(s, rd):
+        if s == 0:
+            rgot[me] = rd
+        else:
+            rback[s - 1] = rd
+            rback_copy(s).start()
+
+    middle(S, S, mixes, combs, stats, inv, full, send, send_stat)
+    backward_kernel(land_own, soft, xs, ys, qs, full, extra)
+    for s in others:
+        back_copy(s).wait_recv()
+        rback_copy(s).wait_recv()
+
+    def final_copy(p, s):
+        return remote(psend.at[p, shift(s)], fbuf.at[s - 1, p], f_s.at[p, s - 1], f_r.at[p, s - 1], shift(s))
+
+    def second(p, carry):
+        cols = lanes(p)
+        second_kernel(
+            q_ref.at[:, cols], k_ref.at[:, cols], v_ref.at[:, cols], g_ref.at[:, cols], lands(p),
+            wf.at[pl.ds(p, 1)], eb.at[pl.ds(p, 1)], got.at[pl.ds(p, 1)], rgot.at[pl.ds(p, 1)],
+            dq.at[:, cols], dk.at[:, cols], gv_ref.at[:, cols], part,
+        )
+        share = jnp.where(p == me, 1.0, 0.0)
+        for i in range(2):
+            sums = (part[i] + share * extra[0, i]).astype(BF16)
+            for d in range(S):
+                psend[p, d, i] = sums[d * land_dev : (d + 1) * land_dev]
+        for s in others:
+            final_copy(p, s).start()
+        return carry
+
+    lax.fori_loop(0, S, second, 0)
+
+    def last(p, carry):
+        for s in others:
+            final_copy(p, s).wait_recv()
+        cols = lanes(p)
+        rows = dq.shape[0]
+        seg = rows // land_dev
+        for i, (src, dst) in enumerate(((dq, gq_ref), (dk, gk_ref))):
+            total = (psend[p, me, i].astype(F32) + sum(fbuf[s - 1, p, i].astype(F32) for s in others)) / seg
+            wide = jnp.broadcast_to(total[:, None, :], (land_dev, seg, PAIR)).reshape(rows, PAIR)
+            dst[:, cols] = (src[:, cols] + wide).astype(BF16)
+        return carry
+
+    lax.fori_loop(0, S, last, 0)
+
+    for i in range(S):
+        for s in others:
+            land_copy(i, s).wait_send()
+            final_copy(i, s).wait_send()
+    for s in others:
+        bundle_copy(s - 1).wait_send()
+        stat_copy(s - 1).wait_send()
+        back_copy(s).wait_send()
+        rback_copy(s).wait_send()
+
+
+def fused(q, k, v, g):
+    rows, width = q.shape
+    S = lax.axis_size("seq")
+    land_dev = M // S
+    V, sem = pltpu.VMEM, pltpu.SemaphoreType.DMA
+    vm = pl.BlockSpec(memory_space=pltpu.VMEM)
+    return pl.pallas_call(
+        functools.partial(whole_kernel, S),
+        out_shape=[shape((rows, width), BF16)] * 3,
+        in_specs=[vm] * 4,
+        out_specs=[vm] * 3,
+        scratch_shapes=[
+            V((2, land_dev, width), BF16),
+            V((S, S, 2, land_dev, PAIR), BF16),
+            V((S, 2 * M, rows), BF16),
+            V((S, 2 * M, rows), BF16),
+            V((S, 2 * M, PAIR), BF16),
+            V((S, 8, M), F32),
+            V((S - 1, 2 * M, PAIR), BF16),
+            V((S - 1, 8, M), F32),
+            V((1, 2, M, M), F32),
+            V((1, 2, ITERS, M, M), F32),
+            V((1, 2, ITERS, M, M), F32),
+            V((1, 2, ITERS, M, M), F32),
+            V((1, 2, M, M), F32),
+            V((1, 3, M, PAIR), F32),
+            V((S - 1, 2 * M, PAIR), BF16),
+            V((S - 1, 8, M), F32),
+            V((S, 2 * M, PAIR), BF16),
+            V((S, 8, M), F32),
+            V((1, 2, M, PAIR), F32),
+            V((rows, width), F32),
+            V((rows, width), F32),
+            V((2, M, PAIR), F32),
+            V((S, S, 2, land_dev, PAIR), BF16),
+            V((S - 1, S, 2, land_dev, PAIR), BF16),
+            sem((S, S - 1)), sem((S, S - 1)),
+            sem((S - 1,)), sem((S - 1,)), sem((S - 1,)), sem((S - 1,)),
+            sem((S - 1,)), sem((S - 1,)), sem((S - 1,)), sem((S - 1,)),
+            sem((S, S - 1)), sem((S, S - 1)),
+        ],
+        compiler_params=pltpu.CompilerParams(vmem_limit_bytes=VMEM_LIMIT, collective_id=0, has_side_effects=True),
+        cost_estimate=cost(2**34, 7 * 2**20),
+    )(q, k, v, g)
+
+
+def per_device(query_rows, key_rows, value_rows, grad_output):
+    data = [x[0] for x in (query_rows, key_rows, value_rows, grad_output)]
+    shared = data[0].shape[1] // PAIR == lax.axis_size("seq")
+    return tuple(x[None] for x in (fused if shared else general)(*data))
 
 
 def solution(mesh):

time: 118 us -> 77.6 us (0.66)
  waiting for transfers between devices: 26.9 us -> 0 us
  starting transfers between devices: 23.9 us -> 0 us
  Pallas kernels: 53.4 us -> 71.8 us
  other arithmetic: 9 us -> 0 us
    ppermute x15 -> x0, waiting for transfers between devices: 26.9 us -> none  [spread_out(): got.append(lax.ppermute(to(lax.rem(me + step, spread)), 'seq', perm))]
    ppermute x15 -> x0, starting transfers between devices: 23.9 us -> none  [spread_out(): got.append(lax.ppermute(to(lax.rem(me + step, spread)), 'seq', perm))]
    pallas_call x7 -> x1, Pallas kernels: 53.4 us -> 71.8 us  [fused(): pl.pallas_call(functools.partial(whole_kernel, S), out_shape=[shape((rows...]
    another operation x10 -> x0, other arithmetic: 5.3 us -> none
    unnamed x4 -> x7, local copies, waits for them, and re-layouts: 0.01 us -> 4.93 us
    dynamic_slice x9 -> x0, local copies, waits for them, and re-layouts: 3.03 us -> none  [the longest x3 2.07 us: to(): return lax.dynamic_index_in_dim(x, d, 0, keepdims=False) if personal else x]
    dynamic_update_slice x1 -> x0, other arithmetic: 1.69 us -> none  [per_device(): part = lax.dynamic_update_slice_in_dim(part, mine, me * PAIR, 2)]
    convert_element_type x1 -> x0, other arithmetic: 1.29 us -> none  [per_device(): part = part.astype(BF16).reshape(2, spread, land_dev, width).swapaxes(0, 1)]
  transfers between devices with their start and end apart: 15 -> 0, of which waited for: 7 -> 0; matrix products, arithmetic and copies ran while one was open for 2% -> 0% of each run, Pallas kernels for 11% -> 0%
where the time goes in v2:
time: 77.6 us; the launch traced here: 77.4 us
  Pallas kernels  71.8 us (93%)
  local copies, waits for them, and re-layouts  4.93 us (6%)
    pallas_call x1, Pallas kernels, fused(): pl.pallas_call(functools.partial(whole_kernel, S), out_shape=[shape((rows...  71.8 us
    unnamed x7, local copies, waits for them, and re-layouts  4.93 us

profile of v2, /device:TPU:0, one launch (start us, length us, event | category | flops | bytes accessed | tf_op | source)
XLA Modules:
  0.0 77.4 jit_solution(7486961716137761230)
XLA Ops:
  0.6 71.8 %shard_map.67 = (bf16[1024,512]{1,0:T(8,128)(2,1)}, bf16[1024,512]{1,0:T(8,128)(2,1)}, bf16[1024,512]{1,0:T(8,128)(2,1)}) custom-call(bf16[1024,512]{1,0:T(8,128)(2,1)} %bitcast.10, bf16[1024,512]{1,0:T(8,128)(2,1)} %bitcast.11, bf16[1024,512]{1,0:T(8,128)(2,1)} %bitcast.12, bf16[1024,512]{1,0:T(8,128)(2,1)} %bitcast.13), custom_call_target="tpu_custom_call" | custom-call | flops 17179869184 | bytes 7340032 | tf_op jit(solution)/shard_map/pallas_call | solution.py:549
  72.4 0.0 copy-start.1
  72.4 2.4 %copy.10 = bf16[1,1024,512]{2,1,0:T(8,128)(2,1)} copy(bf16[1,1024,512]{2,1,0:T(8,128)(2,1)} %bitcast.9) | data formatting | bytes 2097152
  74.8 0.0 copy-done.1
  74.8 0.0 copy-start
  74.8 1.0 %copy.11 = bf16[1,1024,512]{2,1,0:T(8,128)(2,1)} copy(bf16[1,1024,512]{2,1,0:T(8,128)(2,1)S(1)} %bitcast.8) | data formatting | bytes 2097152
  75.8 0.6 copy-done
  76.4 1.0 %copy.12 = bf16[1,1024,512]{2,1,0:T(8,128)(2,1)} copy(bf16[1,1024,512]{2,1,0:T(8,128)(2,1)S(1)} %bitcast.7) | data formatting | bytes 2097152
Async XLA Ops:
  72.4 2.4 %copy-start.1 = (bf16[1024,512]{1,0:T(8,128)(2,1)S(1)}, bf16[1024,512]{1,0:T(8,128)(2,1)}, u32[]{:S(2)}) copy-start(bf16[1024,512]{1,0:T(8,128)(2,1)} %get-tuple-element.7) | copy-start | bytes 3145732
  74.8 1.6 %copy-start = (bf16[1024,512]{1,0:T(8,128)(2,1)S(1)}, bf16[1024,512]{1,0:T(8,128)(2,1)}, u32[]{:S(2)}) copy-start(bf16[1024,512]{1,0:T(8,128)(2,1)} %get-tuple-element.8) | copy-start | bytes 3145732

commit v3 on v2

--- a/solution.py
+++ b/solution.py
@@ -15,20 +15,31 @@
 TEMPER = DH ** (-0.5)
 LOG2 = TEMPER * math.log2(math.e)
 F32, BF16 = jnp.float32, jnp.bfloat16
-HIGH = lax.Precision.HIGH
+HIGH = True
 VMEM_LIMIT = 56 * 1024 * 1024
 
 
-def mm(a, b, prec=None):
-    return lax.dot_general(a, b, (((1,), (0,)), ((), ())), precision=prec, preferred_element_type=F32)
-
-
-def nt(a, b, prec=None):
-    return lax.dot_general(a, b, (((1,), (1,)), ((), ())), precision=prec, preferred_element_type=F32)
-
-
-def tn(a, b, prec=None):
-    return lax.dot_general(a, b, (((0,), (0,)), ((), ())), precision=prec, preferred_element_type=F32)
+def dot(dims, a, b, exact):
+    def one(x, y):
+        return lax.dot_general(x, y, (dims, ((), ())), preferred_element_type=F32)
+
+    if not exact:
+        return one(a, b)
+    ah, bh = a.astype(BF16), b.astype(BF16)
+    al, bl = (a - ah.astype(F32)).astype(BF16), (b - bh.astype(F32)).astype(BF16)
+    return one(ah, bh) + (one(al, bh) + one(ah, bl))
+
+
+def mm(a, b, exact=False):
+    return dot(((1,), (0,)), a, b, exact)
+
+
+def nt(a, b, exact=False):
+    return dot(((1,), (1,)), a, b, exact)
+
+
+def tn(a, b, exact=False):
+    return dot(((0,), (0,)), a, b, exact)
 
 
 def own_half(shape, head):

time: 77.6 us -> 76.3 us (0.983)
  Pallas kernels: 71.8 us -> 70.5 us
    pallas_call x1, Pallas kernels: 71.8 us -> 70.5 us  [fused(): pl.pallas_call(functools.partial(whole_kernel, S), out_shape=[shape((rows...]
where the time goes in v3:
time: 76.3 us; the launch traced here: 76.1 us
  Pallas kernels  70.5 us (92%)
  local copies, waits for them, and re-layouts  4.93 us (6%)
    pallas_call x1, Pallas kernels, fused(): pl.pallas_call(functools.partial(whole_kernel, S), out_shape=[shape((rows...  70.5 us
    unnamed x7, local copies, waits for them, and re-layouts  4.93 us

profile of v3, /device:TPU:0, one launch (start us, length us, event | category | flops | bytes accessed | tf_op | source)
XLA Modules:
  0.0 76.1 jit_solution(5694080552927263833)
XLA Ops:
  0.6 70.5 %shard_map.67 = (bf16[1024,512]{1,0:T(8,128)(2,1)}, bf16[1024,512]{1,0:T(8,128)(2,1)}, bf16[1024,512]{1,0:T(8,128)(2,1)}) custom-call(bf16[1024,512]{1,0:T(8,128)(2,1)} %bitcast.10, bf16[1024,512]{1,0:T(8,128)(2,1)} %bitcast.11, bf16[1024,512]{1,0:T(8,128)(2,1)} %bitcast.12, bf16[1024,512]{1,0:T(8,128)(2,1)} %bitcast.13), custom_call_target="tpu_custom_call" | custom-call | flops 17179869184 | bytes 7340032 | tf_op jit(solution)/shard_map/pallas_call | solution.py:560
  71.1 0.0 copy-start.1
  71.1 2.4 %copy.10 = bf16[1,1024,512]{2,1,0:T(8,128)(2,1)} copy(bf16[1,1024,512]{2,1,0:T(8,128)(2,1)} %bitcast.9) | data formatting | bytes 2097152
  73.5 0.0 copy-done.1
  73.5 0.0 copy-start
  73.5 1.0 %copy.11 = bf16[1,1024,512]{2,1,0:T(8,128)(2,1)} copy(bf16[1,1024,512]{2,1,0:T(8,128)(2,1)S(1)} %bitcast.8) | data formatting | bytes 2097152
  74.5 0.6 copy-done
  75.1 1.0 %copy.12 = bf16[1,1024,512]{2,1,0:T(8,128)(2,1)} copy(bf16[1,1024,512]{2,1,0:T(8,128)(2,1)S(1)} %bitcast.7) | data formatting | bytes 2097152
Async XLA Ops:
  71.1 2.4 %copy-start.1 = (bf16[1024,512]{1,0:T(8,128)(2,1)S(1)}, bf16[1024,512]{1,0:T(8,128)(2,1)}, u32[]{:S(2)}) copy-start(bf16[1024,512]{1,0:T(8,128)(2,1)} %get-tuple-element.7) | copy-start | bytes 3145732
  73.5 1.6 %copy-start = (bf16[1024,512]{1,0:T(8,128)(2,1)S(1)}, bf16[1024,512]{1,0:T(8,128)(2,1)}, u32[]{:S(2)}) copy-start(bf16[1024,512]{1,0:T(8,128)(2,1)} %get-tuple-element.8) | copy-start | bytes 3145732
